TPU v7x, 128 devices: a whole 4x4x4 slice. The times are simulated.
128 devices in a mesh: kv: 32 (over x, z, core), head: 4 (over y).
Axes of the slice: x: 4, y: 4, z: 4, core: 2. Of those that a mesh axis runs over, the one named last changes fastest.
Arguments:
- query_heads: bfloat16 [16, 3, 128, 192], P(None, None, ('kv', 'head')), may hold values from -9 to 9
- key_up: bfloat16 [128, 128, 512], P(('kv', 'head')), may hold values from -0.5 to 0.5
- value_up: bfloat16 [128, 512, 128], P(('kv', 'head')), may hold values from -4 to 4
- output_weight: bfloat16 [16384, 7168], P(('kv', 'head')), may hold values from -0.046875 to 0.046875
- latent_cache: bfloat16 [16, 32768, 576], P(None, 'kv'), may hold values from -400 to 400
- lengths: int32 [16], replicated, may hold values from 32 to 32768, as said below
- positions: int32 [16], replicated, may hold values from 0 to 4095
Outputs:
- attended: bfloat16 [16, 3, 7168], P(None, None, ('kv', 'head'))
Inputs may be any that keep to these rules, and one draw needn't show every extreme that they name: `lengths`: each rollout holds at least 32 filled positions; some rollout holds exactly 32768.
All inputs are finite; a program needn't handle non-finite values.
Results may differ from a plain program's by a relative error of at most 0.022.
Values may be sent and summed in bfloat16 or wider, within the bound.
A program may use at most 256 MiB of HBM per device.

v0:
```python
import jax
import jax.numpy as jnp
from jax import lax
from jax.sharding import PartitionSpec as P

DN = 128
DR = 64
DC = 512


def joined(part, axis, combine):
    gathered = jax.tree.map(lambda a: lax.all_gather(a, axis), part)

    def take(source):
        return jax.tree.map(lambda a: lax.dynamic_index_in_dim(a, source, 0, False), gathered)

    return lax.fori_loop(
        1, lax.axis_size(axis), lambda source, state: combine(state, take(source)), take(0)
    )


def rotate_pairs(vectors, places):
    half_dim = vectors.shape[-1] // 2
    frequency = 10000.0 ** (-jnp.arange(half_dim).astype(vectors.dtype) / half_dim)
    angles = places.astype(vectors.dtype)[..., None] * frequency
    first_half = vectors[..., :half_dim]
    second_half = vectors[..., half_dim:]
    return jnp.concatenate(
        [
            first_half * jnp.cos(angles) - second_half * jnp.sin(angles),
            second_half * jnp.cos(angles) + first_half * jnp.sin(angles),
        ],
        axis=-1,
    )


def join_partials(earlier, later):
    first_top, first_total, first_numer = earlier
    second_top, second_total, second_numer = later
    joint_top = jnp.maximum(first_top, second_top)
    first_factor = jnp.exp(first_top - joint_top)
    second_factor = jnp.exp(second_top - joint_top)
    joint_total = first_total * first_factor + second_total * second_factor
    joint_numer = first_numer * first_factor[..., None] + second_numer * second_factor[..., None]
    return (joint_top, joint_total, joint_numer)


def body(query_heads, key_up, value_up, output_weight, latent_cache, lengths, positions):
    rollouts = query_heads.shape[0]
    new_tokens = query_heads.shape[1]
    heads_mine = query_heads.shape[2]
    model_width = output_weight.shape[1]
    value_width = value_up.shape[2]
    query_latent = jnp.einsum(
        "bshn,hnc->bshc", query_heads[..., :DN], key_up, preferred_element_type=jnp.float32
    )
    places = positions[:, None] + jnp.arange(new_tokens, dtype=jnp.int32)[None, :]
    query_rotary = rotate_pairs(query_heads[..., DN:].astype(jnp.float32), places[:, :, None])
    query_mine = jnp.concatenate([query_latent, query_rotary], axis=-1).astype(jnp.bfloat16)
    query_group = lax.all_gather(query_mine, "kv", axis=2, tiled=True)
    shard_rows = latent_cache.shape[1]
    shard_index = lax.axis_index("kv")
    score_scale = 1.0 / jnp.sqrt(jnp.float32(DN + DR))
    scores = (
        jnp.einsum("bsgd,bjd->bsgj", query_group, latent_cache, preferred_element_type=jnp.float32)
        * score_scale
    )
    slots = shard_index * shard_rows + jnp.arange(shard_rows, dtype=jnp.int32)
    last_visible = lengths[:, None] - new_tokens + jnp.arange(new_tokens, dtype=jnp.int32)[None, :]
    visible = slots[None, None, None, :] <= last_visible[:, :, None, None]
    scores = jnp.where(visible, scores, -1e30)
    local_top = jnp.max(scores, axis=-1)
    weights = jnp.where(visible, jnp.exp(scores - local_top[..., None]), 0.0)
    totals = jnp.sum(weights, axis=-1)
    numerators = jnp.einsum(
        "bsgj,bjc->bsgc",
        weights.astype(jnp.bfloat16),
        latent_cache[..., :DC],
        preferred_element_type=jnp.float32,
    )
    joint_top, joint_total, joint_numer = joined(
        (local_top, totals, numerators), "kv", join_partials
    )
    head_start = shard_index * heads_mine
    mine_numer = lax.dynamic_slice_in_dim(joint_numer, head_start, heads_mine, 2)
    mine_total = lax.dynamic_slice_in_dim(joint_total, head_start, heads_mine, 2)
    latent_out = (mine_numer / mine_total[..., None]).astype(jnp.bfloat16)
    head_values = jnp.einsum(
        "bshc,hcv->bshv", latent_out, value_up, preferred_element_type=jnp.float32
    ).astype(jnp.bfloat16)
    flat_values = head_values.reshape(rollouts * new_tokens, heads_mine * value_width)
    head_term = jnp.dot(flat_values, output_weight, preferred_element_type=jnp.float32)
    head_term = head_term.reshape(rollouts, new_tokens, model_width)
    attended = lax.psum_scatter(head_term, ("kv", "head"), scatter_dimension=2, tiled=True)
    return attended.astype(jnp.bfloat16)


def solution(mesh):
    in_specs = (
        P(None, None, ("kv", "head"), None),
        P(("kv", "head"), None, None),
        P(("kv", "head"), None, None),
        P(("kv", "head"), None),
        P(None, "kv", None),
        P(),
        P(),
    )
    out_specs = P(None, None, ("kv", "head"))
    return jax.shard_map(body, mesh=mesh, in_specs=in_specs, out_specs=out_specs, check_vma=False)
```

profile of v0, /device:TPU:1, one launch (start us, length us, event | category | flops | bytes accessed | tf_op | source)
XLA Modules:
  0.0 620.1 jit_solution(11065752239313542576)
XLA Ops:
  6.5 0.8 slice_convert_fusion
  7.4 0.7 add_convert_fusion
  8.1 1.0 fusion.23
  9.1 0.2 fusion.34
  9.3 0.7 pad_maximum_fusion
  10.1 0.7 broadcast_add_fusion
  10.7 0.1 iota_add_fusion
  10.8 0.1 broadcast_compare_fusion
  10.9 46.6 %all-gather.6.cloned.1.call-done = bf16[16,3,32,576]{3,0,1,2:T(8,128)(2,1)} async-done(((bf16[16,3,1,576]{3,0,1,2:T(8,128)(2,1)}), bf16[16,3,32,576]{3,0,1,2:T(8,128)(2,1)}) %all-gather.6.cloned.1.call-update) | async-done | bytes 1769488 | tf_op jit(solution)/shard_map/all_gather | solution.py:60
  57.5 9.3 %fusion.11 = (f32[16,3,32]{2,1,0:T(4,128)S(1)}, f32[16,3,32,1024]{3,2,1,0:T(8,128)S(1)}) fusion(pred[16,3,1024]{2,1,0:T(4,128)(4,1)S(1)} %broadcast_compare_fusion, bf16[16,1024,576]{1,2,0:T(8,128)(2,1)} %param.13, bf16[16,3,32,576]{3,0,1,2:T(8,128)(2,1)} %all-gather.6.cloned.1.call-done), kind=kOutput, calls=%fused_computation.19 | convolution fusion | flops 1816656384 | bytes 26990592 | tf_op jit(solution)/shard_map/bsgd,bjd->bsgj/dot_general | solution.py:65
  66.9 2.6 copy-done.1
  69.4 10.2 %fusion.8 = f32[16,3,32,512]{3,2,1,0:T(8,128)} fusion(bf16[16,1024,576]{1,2,0:T(8,128)(2,1)} %param.13, f32[16,3,32,1024]{3,2,1,0:T(8,128)S(1)} %get-tuple-element.221, f32[16,3,32]{2,1,0:T(4,128)S(1)} %get-tuple-element.220, pred[16,3,1024]{2,1,0:T(4,128)(4,1)S(1)} %broadcast_compare_fusion), kind=kOutput, calls=%fused_computation.14 | convolution fusion | flops 1618477056 | bytes 26269696 | tf_op jit(solution)/shard_map/bsgj,bjc->bsgc/dot_general | solution.py:75
  79.7 24.8 %all-gather = f32[512,3,32]{2,0,1:T(8,128)S(1)} all-gather(f32[16,3,32]{2,0,1:T(8,128)S(1)} %copy.34), channel_id=2, replica_groups=mesh['kv'=32,'head'=4] {'kv'}, dimensions={0}, use_global_device_ids=true | all-gather | bytes 202752 | tf_op jit(solution)/shard_map/all_gather | solution.py:12
  104.6 4.1 fusion.13
  108.7 23.7 %all-gather.1 = f32[512,3,32]{2,0,1:T(8,128)S(1)} all-gather(f32[16,3,32]{2,0,1:T(8,128)S(1)} %copy.35), channel_id=3, replica_groups=mesh['kv'=32,'head'=4] {'kv'}, dimensions={0}, use_global_device_ids=true | all-gather | bytes 202752 | tf_op jit(solution)/shard_map/all_gather | solution.py:12
  132.4 237.9 %all-gather.8.cloned.1.call-done = f32[512,3,32,512]{3,2,1,0:T(8,128)} async-done(((f32[16,3,32,512]{3,2,1,0:T(8,128)}), f32[512,3,32,512]{3,2,1,0:T(8,128)}) %all-gather.8.cloned.1.call-update) | async-done | bytes 100663312 | tf_op jit(solution)/shard_map/all_gather | solution.py:12
  370.3 4.1 slice.32
  374.3 157.9 %while.19 = (s32[]{:T(128)}, f32[16,3,32]{2,1,0:T(4,128)S(1)}, f32[16,3,32]{2,1,0:T(4,128)S(1)}, f32[16,3,32,512]{3,2,1,0:T(8,128)}, f32[32,16,3,32]{3,1,0,2:T(8...) while((s32[]{:T(128)}, f32[16,3,32]{2,1,0:T(4,128)S(1)}, ...), condition=%wide.region_3.4_spmd, body=%wide.region_2.3_spmd.sunk | while | flops 2368517 | bytes 9523351 | solution.py:17
  374.4 5.0 fusion.47
  379.5 5.0 fusion.47
  384.5 0.1 fusion.46
  384.6 5.0 fusion.47
  389.6 0.1 fusion.46
  389.7 5.0 fusion.47
  394.7 0.1 fusion.46
  394.8 5.0 fusion.47
  399.9 5.0 fusion.47
  405.0 5.0 fusion.47
  410.0 0.1 fusion.46
  410.0 5.0 fusion.47
  415.1 0.1 fusion.46
  415.1 5.0 fusion.47
  420.2 0.1 fusion.46
  420.2 5.0 fusion.47
  425.3 5.0 fusion.47
  430.4 0.1 fusion.46
  430.4 5.0 fusion.47
  435.4 0.1 fusion.46
  435.5 5.0 fusion.47
  440.5 0.1 fusion.46
  440.6 5.0 fusion.47
  445.7 5.0 fusion.47
  450.8 5.0 fusion.47
  455.9 5.0 fusion.47
  461.0 5.0 fusion.47
  466.1 5.0 fusion.47
  471.2 5.0 fusion.47
  476.3 5.0 fusion.47
  481.4 5.0 fusion.47
  486.5 5.0 fusion.47
  491.5 5.0 fusion.47
  496.6 5.0 fusion.47
  501.7 5.0 fusion.47
  506.8 5.0 fusion.47
  511.9 5.0 fusion.47
  517.0 5.0 fusion.47
  522.1 5.0 fusion.47
  527.2 5.0 fusion.47
  532.2 5.4 copy.41
  537.6 0.1 constant_dynamic-slice_fusion.2
  537.7 0.1 copy.42
  537.8 1.5 fusion.21
  539.3 72.6 %all-reduce.2 = bf16[16,3,7168]{2,0,1:T(8,128)(2,1)} all-reduce(f32[16,3,7168]{2,0,1:T(8,128)S(1)} %fusion.21), channel_id=5, replica_groups=mesh['kv'=32,'head'=4] {'kv','head'}, use_global_device_ids=true, to_apply=%region_4.5.clone | all-reduce | flops 344064 | bytes 2064384
  611.9 1.4 dynamic-slice_convert_fusion
  (70 shorter events, 1.8 us)
Async XLA Ops:
  6.5 531.3 %copy-start = (bf16[128,7168]{1,0:T(8,128)(2,1)S(1)}, bf16[128,7168]{1,0:T(8,128)(2,1)}, u32[]{:S(2)}) copy-start(bf16[128,7168]{1,0:T(8,128)(2,1)} %param.12) | copy-start | bytes 5505028
  6.5 51.0 %all-gather.6.cloned.1.call-start = ((), (), s32[]{:S(2)}) async-start(), calls=%async_computation | async-start | bytes 2027520 | tf_op jit(solution)/shard_map/all_gather | solution.py:60
  10.0 360.3 %all-gather.8.cloned.1.call-start = ((), (), s32[]{:S(2)}) async-start(), calls=%async_computation.1 | async-start | bytes 103809024 | tf_op jit(solution)/shard_map/all_gather | solution.py:12
  66.9 2.6 copy-start.1
  532.2 5.6 copy-start.2
Sparse Core Ops, SparseCore 0:
  10.1 47.3 all-gather.5
  79.8 290.4 all-gather.7
where the time goes:
time: 620 us
  waiting for transfers between devices  284 us (46%)
  other arithmetic  165 us (27%)
  blocking collectives  121 us (20%)
  matrix products  22 us (4%)
  local copies, waits for them, and re-layouts  13.8 us (2%)
  between operations  13.5 us (2%)
    all_gather x1, waiting for transfers between devices, joined(): gathered = jax.tree.map(lambda a: lax.all_gather(a, axis), part)  238 us
    add x31, other arithmetic, join_partials(): first_numer * first_factor[..., None]  156 us
    unnamed x1, blocking collectives  72.6 us
    all_gather x2, blocking collectives, joined(): gathered = jax.tree.map(lambda a: lax.all_gather(a, axis), part)  48.5 us
    all_gather x1, waiting for transfers between devices, body(): query_group = lax.all_gather(query_mine, 'kv', axis=2, tiled=True)  46.6 us
  transfers between devices with their start and end apart: 2, of which 2 were waited for; matrix products, arithmetic and copies ran while one was open for 1% of the time, Pallas kernels for 0%

commit v1 on v0

--- a/solution.py
+++ b/solution.py
@@ -6,17 +6,6 @@
 DN = 128
 DR = 64
 DC = 512
-
-
-def joined(part, axis, combine):
-    gathered = jax.tree.map(lambda a: lax.all_gather(a, axis), part)
-
-    def take(source):
-        return jax.tree.map(lambda a: lax.dynamic_index_in_dim(a, source, 0, False), gathered)
-
-    return lax.fori_loop(
-        1, lax.axis_size(axis), lambda source, state: combine(state, take(source)), take(0)
-    )
 
 
 def rotate_pairs(vectors, places):
@@ -32,17 +21,6 @@
         ],
         axis=-1,
     )
-
-
-def join_partials(earlier, later):
-    first_top, first_total, first_numer = earlier
-    second_top, second_total, second_numer = later
-    joint_top = jnp.maximum(first_top, second_top)
-    first_factor = jnp.exp(first_top - joint_top)
-    second_factor = jnp.exp(second_top - joint_top)
-    joint_total = first_total * first_factor + second_total * second_factor
-    joint_numer = first_numer * first_factor[..., None] + second_numer * second_factor[..., None]
-    return (joint_top, joint_total, joint_numer)
 
 
 def body(query_heads, key_up, value_up, output_weight, latent_cache, lengths, positions):
@@ -69,21 +47,20 @@
     last_visible = lengths[:, None] - new_tokens + jnp.arange(new_tokens, dtype=jnp.int32)[None, :]
     visible = slots[None, None, None, :] <= last_visible[:, :, None, None]
     scores = jnp.where(visible, scores, -1e30)
-    local_top = jnp.max(scores, axis=-1)
-    weights = jnp.where(visible, jnp.exp(scores - local_top[..., None]), 0.0)
+    top = lax.pmax(jnp.max(scores, axis=-1), "kv")
+    weights = jnp.where(visible, jnp.exp(scores - top[..., None]), 0.0)
     totals = jnp.sum(weights, axis=-1)
     numerators = jnp.einsum(
-        "bsgj,bjc->bsgc",
+        "bsgj,bjc->gbsc",
         weights.astype(jnp.bfloat16),
         latent_cache[..., :DC],
         preferred_element_type=jnp.float32,
     )
-    joint_top, joint_total, joint_numer = joined(
-        (local_top, totals, numerators), "kv", join_partials
-    )
+    mine_numer = lax.psum_scatter(numerators, "kv", scatter_dimension=0, tiled=True)
+    joint_total = lax.psum(totals, "kv")
     head_start = shard_index * heads_mine
-    mine_numer = lax.dynamic_slice_in_dim(joint_numer, head_start, heads_mine, 2)
     mine_total = lax.dynamic_slice_in_dim(joint_total, head_start, heads_mine, 2)
+    mine_numer = jnp.transpose(mine_numer, (1, 2, 0, 3))
     latent_out = (mine_numer / mine_total[..., None]).astype(jnp.bfloat16)
     head_values = jnp.einsum(
         "bshc,hcv->bshv", latent_out, value_up, preferred_element_type=jnp.float32

time: 620 us -> 420 us (0.68)
  waiting for transfers between devices: 284 us -> 46.6 us
  blocking collectives: 121 us -> 320 us
  other arithmetic: 165 us -> 7.37 us
  local copies, waits for them, and re-layouts: 13.8 us -> 5.13 us
    all_gather x1 -> x0, waiting for transfers between devices: 238 us -> none  [joined(): gathered = jax.tree.map(lambda a: lax.all_gather(a, axis), part)]
    add x62 -> x0, other arithmetic: 158 us -> none  [the longest x31 156 us: join_partials(): first_numer * first_factor[..., None]]
    psum x0 -> x1, blocking collectives: none -> 124 us  [body(): joint_total = lax.psum(totals, 'kv')]
    pmax x0 -> x1, blocking collectives: none -> 121 us  [body(): top = lax.pmax(jnp.max(scores, axis=-1), 'kv')]
    all_gather x2 -> x0, blocking collectives: 48.5 us -> none  [joined(): gathered = jax.tree.map(lambda a: lax.all_gather(a, axis), part)]
  transfers between devices with their start and end apart: 2 -> 2, of which waited for: 2 -> 1; matrix products, arithmetic and copies ran while one was open for 1% -> 1% of each run, Pallas kernels for 0% -> 0%
where the time goes in v1:
time: 420 us
  blocking collectives  320 us (76%)
  waiting for transfers between devices  46.6 us (11%)
  matrix products  26.9 us (6%)
  between operations  13.5 us (3%)
  other arithmetic  7.37 us (2%)
  local copies, waits for them, and re-layouts  5.13 us (1%)
    psum x1, blocking collectives, body(): joint_total = lax.psum(totals, 'kv')  124 us
    pmax x1, blocking collectives, body(): top = lax.pmax(jnp.max(scores, axis=-1), 'kv')  121 us
    unnamed x1, blocking collectives  75.6 us
    all_gather x1, waiting for transfers between devices, body(): query_group = lax.all_gather(query_mine, 'kv', axis=2, tiled=True)  46.6 us
    dot_general x1, matrix products, body(): jnp.einsum('bsgd,bjd->bsgj', query_group, latent_cache, preferred_element...  14 us
    dot_general x1, matrix products, body(): jnp.einsum('bsgj,bjc->gbsc', weights.astype(jnp.bfloat16), latent_cache[....  10.4 us
  transfers between devices with their start and end apart: 2, of which 1 were waited for; matrix products, arithmetic and copies ran while one was open for 1% of the time, Pallas kernels for 0%

profile of v1, /device:TPU:1, one launch (start us, length us, event | category | flops | bytes accessed | tf_op | source)
XLA Modules:
  0.0 420.0 jit_solution(4388134731512568879)
XLA Ops:
  6.5 0.0 copy-start
  6.5 0.0 all-gather.2.cloned.1.call-start
  6.5 0.8 slice_convert_fusion
  7.4 0.7 add_convert_fusion
  8.1 1.0 fusion.22
  9.1 0.2 fusion.33
  9.3 0.7 pad_maximum_fusion
  10.0 0.0 all-gather.2.cloned.1.call-update
  10.0 0.0 reduce-scatter.3.cloned.1.call-start
  10.1 0.7 broadcast_add_fusion
  10.7 0.1 iota_add_fusion
  10.8 0.1 broadcast_compare_fusion
  10.9 46.6 %all-gather.2.cloned.1.call-done = bf16[16,3,32,576]{3,0,1,2:T(8,128)(2,1)} async-done(((bf16[16,3,1,576]{3,0,1,2:T(8,128)(2,1)}), bf16[16,3,32,576]{3,0,1,2:T(8,128)(2,1)}) %all-gather.2.cloned.1.call-update) | async-done | bytes 1769488 | tf_op jit(solution)/shard_map/all_gather | solution.py:38
  57.5 14.0 %fusion.5 = (f32[16,3,32]{2,1,0:T(4,128)S(1)}, f32[16,3,32,1024]{3,2,1,0:T(8,128)}) fusion(pred[16,3,1024]{2,1,0:T(4,128)(4,1)S(1)} %broadcast_compare_fusion, bf16[16,1024,576]{1,2,0:T(8,128)(2,1)} %param.11, bf16[16,3,32,576]{3,0,1,2:T(8,128)(2,1)} %all-gather.2.cloned.1.call-done), kind=kOutput, calls=%fused_computation.7 | convolution fusion | flops 1816656384 | bytes 26990592 | tf_op jit(solution)/shard_map/bsgd,bjd->bsgj/dot_general | solution.py:43
  71.5 120.9 %pmax.7 = f32[16,3,32]{2,1,0:T(4,128)S(1)} all-reduce(f32[16,3,32]{2,1,0:T(4,128)S(1)} %get-tuple-element.7), channel_id=1, replica_groups=mesh['kv'=32,'head'=4] {'kv'}, use_global_device_ids=true, to_apply=%region_1.2 | all-reduce | flops 1536 | bytes 12288 | tf_op jit(solution)/shard_map/pmax | solution.py:50
  192.4 10.4 %fusion.15 = f32[32,16,3,512]{3,0,2,1:T(8,128)S(1)} fusion(bf16[16,1024,576]{1,2,0:T(8,128)(2,1)} %param.11, f32[16,3,32,1024]{3,2,1,0:T(8,128)} %get-tuple-element.8, f32[16,3,32]{2,1,0:T(4,128)S(1)} %pmax.7, pred[16,3,1024]{2,1,0:T(4,128)(4,1)S(1)} %broadcast_compare_fusion), kind=kOutput, calls=%fused_computation.16 | convolution fusion | flops 1618477056 | bytes 26269696 | tf_op jit(solution)/shard_map/bsgj,bjc->gbsc/dot_general | solution.py:53
  202.8 3.5 copy.23
  206.3 0.0 copy-start.1
  206.3 0.0 reduce-scatter.3.cloned.1.call-update
  206.3 4.1 fusion.6
  210.5 124.0 %psum.7 = f32[16,3,32]{2,1,0:T(4,128)S(1)} all-reduce(f32[16,3,32]{2,1,0:T(4,128)S(1)} %fusion.6), channel_id=1, replica_groups=mesh['kv'=32,'head'=4] {'kv'}, use_global_device_ids=true, to_apply=%region_4.5 | all-reduce | flops 1536 | bytes 12288 | tf_op jit(solution)/shard_map/psum | solution.py:60
  334.4 0.1 constant_dynamic-slice_fusion
  334.5 0.1 copy.24
  334.6 0.0 reduce-scatter.3.cloned.1.call-done
  334.6 0.0 copy-done
  334.6 0.0 copy-done.1
  334.6 1.5 fusion.20
  336.1 75.6 %all-reduce.2 = bf16[16,3,7168]{2,0,1:T(8,128)(2,1)} all-reduce(f32[16,3,7168]{2,0,1:T(8,128)S(1)} %fusion.20), channel_id=3, replica_groups=mesh['kv'=32,'head'=4] {'kv','head'}, use_global_device_ids=true, to_apply=%region_5.6.clone | all-reduce | flops 344064 | bytes 2064384
  411.7 1.4 dynamic-slice_convert_fusion
  (2 shorter events, 0.0 us)
Async XLA Ops:
  6.5 328.1 %copy-start = (bf16[128,7168]{1,0:T(8,128)(2,1)S(1)}, bf16[128,7168]{1,0:T(8,128)(2,1)}, u32[]{:S(2)}) copy-start(bf16[128,7168]{1,0:T(8,128)(2,1)} %param.10) | copy-start | bytes 5505028
  6.5 51.0 %all-gather.2.cloned.1.call-start = ((), (), s32[]{:S(2)}) async-start(), calls=%async_computation.1 | async-start | bytes 2027520 | tf_op jit(solution)/shard_map/all_gather | solution.py:38
  10.0 324.6 %reduce-scatter.3.cloned.1.call-start = ((), (), s32[]{:S(2)}) async-start(), calls=%async_computation.2 | async-start | bytes 3244032 | tf_op jit(solution)/shard_map/reduce_scatter | solution.py:59
  206.3 128.3 %copy-start.1 = (bf16[1,512,128]{2,1,0:T(8,128)(2,1)S(1)}, bf16[1,512,128]{2,1,0:T(8,128)(2,1)}, u32[]{:S(2)}) copy-start(bf16[1,512,128]{2,1,0:T(8,128)(2,1)} %param.9) | copy-start | bytes 393220
Sparse Core Ops, SparseCore 0:
  10.1 47.3 all-gather.1
  206.5 80.3 reduce-scatter.2

commit v2 on v1

v2 whole, which is shorter than its diff:
```python
import functools

import jax
import jax.numpy as jnp
import numpy as np
from jax import lax
from jax.experimental import pallas as pl
from jax.experimental.pallas import tpu as pltpu
from jax.sharding import PartitionSpec as P

MESH = pl.DeviceIdType.MESH
BF = jnp.bfloat16
F32 = jnp.float32

DN = 128
DR = 64
DC = 512
B = 16
S = 3
ROWS = B * S
CHUNKS = ROWS // 16
RANK = DC + DR
WIDE = 640
SHARD = 1024
FEAT = 56
MASKED = -(2.0**100)
FACTOR = float(np.log2(np.e) / np.sqrt(DN + DR))

dot = functools.partial(lax.dot_general, preferred_element_type=F32)
NN = (((1,), (0,)), ((), ()))
NT = (((1,), (1,)), ((), ()))


def split3(value):
    high = value.astype(BF).astype(F32)
    rest = value - high
    middle = rest.astype(BF).astype(F32)
    return high, middle, rest - middle


def stat_tile(top, total):
    lane = lax.broadcasted_iota(jnp.int32, (top.shape[0], 128), 1)
    top_high, top_middle, top_low = split3(top)
    total_high, total_middle, _ = split3(total)
    tile = jnp.where(lane == 4, total_middle, 0.0)
    tile = jnp.where(lane == 3, total_high, tile)
    tile = jnp.where(lane == 2, top_low, tile)
    tile = jnp.where(lane == 1, top_middle, tile)
    return jnp.where(lane == 0, top_high, tile)


def spread_stats(tile):
    source = lax.broadcasted_iota(jnp.int32, (128, 256), 0)
    target = lax.broadcasted_iota(jnp.int32, (128, 256), 1)
    is_top = (source < 3) & (target < 128)
    is_total = (source >= 3) & (source < 5) & (target >= 128)
    spread = jnp.where(is_top | is_total, 1.0, 0.0).astype(BF)
    both = dot(tile.astype(BF), spread, NN)
    return both[:, :128], both[:, 128:]


def join(parts):
    stats = [spread_stats(tile) for _, tile in parts]
    top = functools.reduce(jnp.maximum, [m for m, _ in stats])
    factors = [jnp.exp2((m - top) * FACTOR) for m, _ in stats]
    total = sum(f * l for f, (_, l) in zip(factors, stats))
    tiles = []
    for t in range(DC // 128):
        tiles.append(sum(f * data(t) for f, (data, _) in zip(factors, parts)))
    return tiles, top, total


def block_part(ref, index, count):
    rows = count * 16

    def data(t):
        return ref[index][..., 128 * t : 128 * t + 128].astype(F32).reshape(rows, 128)

    return data, ref[index][..., DC:WIDE].reshape(rows, 128)


def kernel(
    lengths_ref, positions_ref, query_ref, key_ref, value_ref, weight_hbm, cache_hbm, out_ref,
    cache, weight, wide, wide_sib, gathered, query_f32, scores_a, scores_b, probs_a, probs_b,
    stats_a, stats_b, partial, pair_send, pair_recv, first_send, first_recv, second_send, second_recv,
    latent, values, values_sib, out_send, out_first, out_mid, out_second, out_pairs, out_third,
    cache_sem, weight_sem, g1_send, g1_recv, g2_send, g2_recv, g3_send, g3_recv, g4_send, g4_recv,
    pair_ss, pair_rs, r1_send, r1_recv, r2_send, r2_recv, w_send, w_recv, v_send, v_recv,
    o1_send, o1_recv, o2_send, o2_recv, o3_send, o3_recv,
):
    kv = lax.axis_index("kv")
    row_y = lax.axis_index("head")
    x, z, core = kv // 8, (kv // 2) % 4, kv % 2

    def place(px, pz, pc, py):
        return (lax.rem(px, 4) * 8 + lax.rem(pz, 4) * 2 + pc, lax.rem(py, 4))

    def along_first(step):
        return place(x + step * (1 - core), z + step * core, core, row_y)

    def along_second(step):
        return place(x + step * core, z + step * (1 - core), core, row_y)

    def along_third(step):
        return place(x, z, core, row_y + step)

    sibling = place(x, z, 1 - core, row_y)

    def remote(src, dst, send, recv, device):
        return pltpu.make_async_remote_copy(
            src_ref=src, dst_ref=dst, send_sem=send, recv_sem=recv,
            device_id=device, device_id_type=MESH,
        )

    def cache_copy(b):
        return pltpu.make_async_copy(cache_hbm.at[b], cache.at[b], cache_sem.at[b])

    weight_copy = pltpu.make_async_copy(weight_hbm, weight, weight_sem.at[0])

    barrier = pltpu.get_barrier_semaphore()
    partners = [sibling]
    for step in range(1, 4):
        partners += [along_first(step), along_second(step), along_third(step)]
    for partner in partners:
        pl.semaphore_signal(barrier, inc=1, device_id=partner, device_id_type=MESH)
    weight_copy.start()
    for b in range(B):
        cache_copy(b).start()

    line = lax.broadcasted_iota(jnp.int32, (ROWS, ROWS), 0)
    column = lax.broadcasted_iota(jnp.int32, (ROWS, ROWS), 1)
    reorder = jnp.where(column == (line % S) * B + line // S, 1.0, 0.0).astype(BF)
    query = dot(reorder, query_ref[...], NN)
    query_latent = dot(query[:, :DN].astype(BF), key_ref[...], NN)
    lane = lax.broadcasted_iota(jnp.int32, (ROWS, DR // 2), 1).astype(F32)
    frequency = jnp.exp(lane * (-np.log(10000.0) / (DR // 2)))
    token_row = lax.broadcasted_iota(jnp.int32, (ROWS, DR // 2), 0)
    spot = jnp.zeros((ROWS, DR // 2), jnp.int32)
    for b in range(B):
        spot = jnp.where(token_row // S == b, positions_ref[b], spot)
    angle = (spot + token_row % S).astype(F32) * frequency
    cosine, sine = jnp.cos(angle), jnp.sin(angle)
    first_half, second_half = query[:, DN : DN + DR // 2], query[:, DN + DR // 2 :]
    own = jnp.concatenate(
        [
            query_latent,
            first_half * cosine - second_half * sine,
            second_half * cosine + first_half * sine,
            jnp.zeros((ROWS, WIDE - RANK), F32),
        ],
        axis=1,
    ).astype(BF)
    for k in range(CHUNKS):
        gathered[0, k, 0] = own[16 * k : 16 * k + 16]

    pl.semaphore_wait(barrier, len(partners))

    def gather_one(k, step):
        return remote(
            gathered.at[0, k, 0], gathered.at[0, k, step],
            g1_send.at[k, step - 1], g1_recv.at[k, step - 1], along_first(step),
        )

    def gather_two(k, side):
        return remote(
            gathered.at[0, k, pl.ds(0, 4)], gathered.at[0, k, pl.ds(4 if side == 0 else 12, 4)],
            g2_send.at[k, side], g2_recv.at[k, side], along_second(1 if side == 0 else 3),
        )

    def gather_three(k, side):
        return remote(
            gathered.at[0, k, pl.ds(4 if side == 0 else 14, 2)],
            gathered.at[0, k, pl.ds(8 if side == 0 else 10, 2)],
            g3_send.at[k, side], g3_recv.at[k, side], along_second(1 if side == 0 else 3),
        )

    def gather_four(k):
        return remote(gathered.at[0, k], gathered.at[1, k], g4_send.at[k], g4_recv.at[k], sibling)

    for k in range(CHUNKS):
        for step in range(1, 4):
            gather_one(k, step).start()

    weight_copy.wait()

    def widen(g, carry):
        base = pl.multiple_of(g * (16 * FEAT), 128)
        strip = weight[:, pl.ds(base, 16 * FEAT)]
        gap = jnp.zeros((DN, 64 - FEAT), BF)
        for low in range(2):
            wx, wz = g // 2, (g % 2) * 2 + low
            for parity in range(2):
                slot = wz * 4 + wx if parity == 0 else wx * 4 + wz
                for half in range(2):
                    start = ((low * 2 + parity) * 4 + half * 2) * FEAT
                    wide[parity, slot, :, 128 * half : 128 * half + 128] = jnp.concatenate(
                        [strip[:, start : start + FEAT], gap,
                         strip[:, start + FEAT : start + 2 * FEAT], gap], axis=1)
        return carry

    lax.fori_loop(0, 8, widen, 0)
    weight_send = remote(wide.at[1 - core], wide_sib, w_send.at[0], w_recv.at[0], sibling)

    for k in range(CHUNKS):
        for step in range(1, 4):
            gather_one(k, step).wait_recv()
        for side in range(2):
            gather_two(k, side).start()
    for k in range(CHUNKS):
        for side in range(2):
            gather_two(k, side).wait_recv()
            gather_three(k, side).start()
    for k in range(CHUNKS):
        for side in range(2):
            gather_three(k, side).wait_recv()
        gather_four(k).start()
    weight_send.start()

    def unpack(k):
        for parity in range(2):
            for t in range(WIDE // 128):
                query_f32[k, t, parity * 256 : parity * 256 + 256] = (
                    gathered[parity, k, :, :, 128 * t : 128 * t + 128].astype(F32).reshape(256, 128)
                )

    for k in range(CHUNKS):
        gather_four(k).wait_recv()
        unpack(k)

    slots = lax.broadcasted_iota(jnp.int32, (1, SHARD), 1)

    def score(b, target):
        rows = []
        for s in range(S):
            r = b * S + s
            tiles = [
                query_f32[r // 16, t, pl.ds(r % 16, 32, stride=16), :] for t in range(WIDE // 128)
            ]
            rows.append(jnp.concatenate(tiles, axis=1)[:, :RANK])
        target[...] = dot(jnp.concatenate(rows, axis=0).astype(BF), cache[b], NN)

    def soften(b, source, target, stats):
        for s in range(S):
            last = lengths_ref[b] - S + s - kv * SHARD
            part = jnp.where(slots <= last, source[32 * s : 32 * s + 32, :], MASKED)
            top = jnp.max(part, axis=1, keepdims=True)
            weights = jnp.exp2((part - top) * FACTOR)
            total = jnp.sum(weights, axis=1, keepdims=True)
            target[32 * s : 32 * s + 32, :] = weights.astype(BF)
            stats[32 * s : 32 * s + 32, :] = stat_tile(top, total)

    def weigh(b, source, stats):
        numerators = dot(source[...], cache[b, :DC], NT)
        for s in range(S):
            r = b * S + s
            for t in range(DC // 128):
                partial[r // 16, t, pl.ds(r % 16, 32, stride=16), :] = numerators[
                    32 * s : 32 * s + 32, 128 * t : 128 * t + 128
                ]
            partial[r // 16, 4, pl.ds(r % 16, 32, stride=16), :] = stats[32 * s : 32 * s + 32, :]

    def pair_copy(k):
        return remote(pair_send.at[k], pair_recv.at[k], pair_ss.at[k], pair_rs.at[k], sibling)

    def first_copy(k, step):
        return remote(
            first_send.at[k, pl.ds(4 * step, 4)], first_recv.at[k, step - 1],
            r1_send.at[k, step - 1], r1_recv.at[k, step - 1], along_second(4 - step),
        )

    def second_copy(k, step):
        return remote(
            second_send.at[k, step], second_recv.at[k, step - 1],
            r2_send.at[k, step - 1], r2_recv.at[k, step - 1], along_first(4 - step),
        )

    def step_pair(k):
        for t in range(WIDE // 128):
            pair_send[k, :, :, 128 * t : 128 * t + 128] = (
                partial[k, t, 256:512].astype(BF).reshape(16, 16, 128)
            )
        pair_copy(k).start()

    def step_first(k):
        pair_copy(k).wait_recv()
        for group in range(4):
            rows = slice(64 * group, 64 * group + 64)
            own_part = (lambda t, rows=rows: partial[k, t, rows], partial[k, 4, rows])
            span = slice(4 * group, 4 * group + 4)
            store_group(k, group, join([own_part, block_part(pair_recv, (k, span), 4)]))
        for step in (2, 1, 3):
            first_copy(k, step).start()

    def store_group(k, group, joined):
        tiles, top, total = joined
        tiles = tiles + [stat_tile(top, total)]
        for t in range(WIDE // 128):
            first_send[k, 4 * group : 4 * group + 4, :, 128 * t : 128 * t + 128] = (
                tiles[t].astype(BF).reshape(4, 16, 128)
            )

    def step_second(k):
        for step in range(1, 4):
            first_copy(k, step).wait_recv()
        parts = [block_part(first_send, (k, slice(0, 4)), 4)]
        parts += [block_part(first_recv, (k, step), 4) for step in range(3)]
        tiles, top, total = join(parts)
        tiles = tiles + [stat_tile(top, total)]
        for t in range(WIDE // 128):
            second_send[k, :, :, 128 * t : 128 * t + 128] = tiles[t].astype(BF).reshape(4, 16, 128)
        for step in (2, 1, 3):
            second_copy(k, step).start()

    def step_last(k):
        for step in range(1, 4):
            second_copy(k, step).wait_recv()
        parts = [block_part(second_send, (k, 0), 1)]
        parts += [block_part(second_recv, (k, step), 1) for step in range(3)]
        tiles, _, total = join(parts)
        for t in range(DC // 128):
            latent[16 * k : 16 * k + 16, 128 * t : 128 * t + 128] = (tiles[t] / total).astype(BF)

    cache_copy(0).wait()
    score(0, scores_a)
    soften(0, scores_a, probs_a, stats_a)

    def after(b, schedule):
        for when, step, k in schedule:
            pl.when(b == when)(functools.partial(step, k))

    def rollout_pair(i, carry):
        b = 2 * i
        cache_copy(b + 1).wait()
        cache_copy(b + 2).wait()
        score(b + 1, scores_b)
        weigh(b, probs_a, stats_a)
        soften(b + 1, scores_b, probs_b, stats_b)
        after(b, [(10, step_pair, 1), (12, step_first, 1)])
        score(b + 2, scores_a)
        weigh(b + 1, probs_b, stats_b)
        soften(b + 2, scores_a, probs_a, stats_a)
        after(b + 1, [(5, step_pair, 0), (7, step_first, 0), (9, step_second, 0), (13, step_last, 0)])
        return carry

    lax.fori_loop(0, B // 2 - 1, rollout_pair, 0)
    cache_copy(B - 1).wait()
    score(B - 1, scores_b)
    weigh(B - 2, probs_a, stats_a)
    soften(B - 1, scores_b, probs_b, stats_b)
    step_second(1)
    weigh(B - 1, probs_b, stats_b)
    step_pair(2)
    step_last(1)
    step_first(2)
    step_second(2)
    step_last(2)

    head_values = dot(latent[...], value_ref[...], NN).astype(BF)
    back = jnp.where(line == (column % S) * B + column // S, 1.0, 0.0).astype(BF)
    values[...] = dot(back, head_values, NN).astype(BF)
    values_copy = remote(values, values_sib, v_send.at[0], v_recv.at[0], sibling)
    values_copy.start()
    weight_send.wait_recv()
    values_copy.wait_recv()

    own_second = x * core + z * (1 - core)
    own_first = x * (1 - core) + z * core
    both_values = jnp.concatenate([values[...], values_sib[...]], axis=1)

    def project(t, carry):
        both_weights = jnp.concatenate([wide[core, t], wide_sib[t]], axis=0)
        out_send[t] = dot(both_values, both_weights, NN).astype(BF)
        return carry

    lax.fori_loop(0, 16, project, 0)

    def out_one(step):
        return remote(
            out_send.at[pl.ds(4 * lax.rem(own_second + step, 4), 4)], out_first.at[step - 1],
            o1_send.at[step - 1], o1_recv.at[step - 1], along_second(step),
        )

    def out_two(step):
        return remote(
            out_mid.at[lax.rem(own_first + step, 4)], out_second.at[step - 1],
            o2_send.at[step - 1], o2_recv.at[step - 1], along_first(step),
        )

    def out_three(step):
        return remote(
            out_pairs.at[lax.rem(row_y + step, 4) // 2], out_third.at[step - 1],
            o3_send.at[step - 1], o3_recv.at[step - 1], along_third(step),
        )

    for step in (2, 1, 3):
        out_one(step).start()
    for step in range(1, 4):
        out_one(step).wait_recv()
    for f in range(4):
        total = out_send[own_second * 4 + f].astype(F32)
        for step in range(3):
            total = total + out_first[step, f].astype(F32)
        out_mid[f] = total.astype(BF)
    for step in (2, 1, 3):
        out_two(step).start()
    for step in range(1, 4):
        out_two(step).wait_recv()
    total = out_mid[own_first].astype(F32)
    for step in range(3):
        total = total + out_second[step].astype(F32)
    out_pairs[0] = total[:, :128].astype(BF)
    out_pairs[1] = total[:, 128:].astype(BF)
    for step in (2, 1, 3):
        out_three(step).start()
    for step in range(1, 4):
        out_three(step).wait_recv()
    total = out_pairs[row_y // 2].astype(F32)
    for step in range(3):
        total = total + out_third[step].astype(F32)
    mine = jnp.where(row_y % 2 == 0, total[:, :FEAT], total[:, 64 : 64 + FEAT])
    out_ref[...] = mine.astype(BF)

    for k in range(CHUNKS):
        for step in range(1, 4):
            gather_one(k, step).wait_send()
            first_copy(k, step).wait_send()
            second_copy(k, step).wait_send()
        for side in range(2):
            gather_two(k, side).wait_send()
            gather_three(k, side).wait_send()
        gather_four(k).wait_send()
        pair_copy(k).wait_send()
    weight_send.wait_send()
    values_copy.wait_send()
    for step in range(1, 4):
        out_one(step).wait_send()
        out_two(step).wait_send()
        out_three(step).wait_send()


def body(query_heads, key_up, value_up, output_weight, latent_cache, lengths, positions):
    query = jnp.transpose(query_heads[:, :, 0, :], (1, 0, 2)).reshape(ROWS, DN + DR)
    cache = jnp.swapaxes(latent_cache, 1, 2)
    width = output_weight.shape[1]
    dma = pltpu.SemaphoreType.DMA
    vmem, smem = pltpu.VMEM, pltpu.SMEM
    out = pl.pallas_call(
        kernel,
        out_shape=jax.ShapeDtypeStruct((ROWS, FEAT), BF),
        in_specs=[
            pl.BlockSpec(memory_space=smem),
            pl.BlockSpec(memory_space=smem),
            pl.BlockSpec(memory_space=vmem),
            pl.BlockSpec(memory_space=vmem),
            pl.BlockSpec(memory_space=vmem),
            pl.BlockSpec(memory_space=pl.ANY),
            pl.BlockSpec(memory_space=pl.ANY),
        ],
        out_specs=pl.BlockSpec(memory_space=vmem),
        scratch_shapes=[
            vmem((B, RANK, SHARD), BF),
            vmem((DN, width), BF),
            vmem((2, 16, DN, 256), BF),
            vmem((16, DN, 256), BF),
            vmem((2, CHUNKS, 16, 16, WIDE), BF),
            vmem((CHUNKS, WIDE // 128, 512, 128), F32),
            vmem((96, SHARD), F32),
            vmem((96, SHARD), F32),
            vmem((96, SHARD), BF),
            vmem((96, SHARD), BF),
            vmem((96, 128), F32),
            vmem((96, 128), F32),
            vmem((CHUNKS, WIDE // 128, 512, 128), F32),
            vmem((CHUNKS, 16, 16, WIDE), BF),
            vmem((CHUNKS, 16, 16, WIDE), BF),
            vmem((CHUNKS, 16, 16, WIDE), BF),
            vmem((CHUNKS, 3, 4, 16, WIDE), BF),
            vmem((CHUNKS, 4, 16, WIDE), BF),
            vmem((CHUNKS, 3, 16, WIDE), BF),
            vmem((ROWS, DC), BF),
            vmem((ROWS, 128), BF),
            vmem((ROWS, 128), BF),
            vmem((16, ROWS, 256), BF),
            vmem((3, 4, ROWS, 256), BF),
            vmem((4, ROWS, 256), BF),
            vmem((3, ROWS, 256), BF),
            vmem((2, ROWS, 128), BF),
            vmem((3, ROWS, 128), BF),
            dma((B,)),
            dma((1,)),
            dma((CHUNKS, 3)), dma((CHUNKS, 3)),
            dma((CHUNKS, 2)), dma((CHUNKS, 2)),
            dma((CHUNKS, 2)), dma((CHUNKS, 2)),
            dma((CHUNKS,)), dma((CHUNKS,)),
            dma((CHUNKS,)), dma((CHUNKS,)),
            dma((CHUNKS, 3)), dma((CHUNKS, 3)),
            dma((CHUNKS, 3)), dma((CHUNKS, 3)),
            dma((1,)), dma((1,)),
            dma((1,)), dma((1,)),
            dma((3,)), dma((3,)),
            dma((3,)), dma((3,)),
            dma((3,)), dma((3,)),
        ],
        compiler_params=pltpu.CompilerParams(
            collective_id=0, has_side_effects=True, vmem_limit_bytes=56 * 2**20
        ),
    )(lengths, positions, query, key_up[0], value_up[0], output_weight, cache)
    return jnp.transpose(out.reshape(S, B, FEAT), (1, 0, 2))


def solution(mesh):
    in_specs = (
        P(None, None, ("kv", "head"), None),
        P(("kv", "head"), None, None),
        P(("kv", "head"), None, None),
        P(("kv", "head"), None),
        P(None, "kv", None),
        P(),
        P(),
    )
    out_specs = P(None, None, ("kv", "head"))
    return jax.shard_map(body, mesh=mesh, in_specs=in_specs, out_specs=out_specs, check_vma=False)
```

time: 420 us -> 77.3 us (0.18)
  blocking collectives: 320 us -> 0 us
  Pallas kernels: 0 us -> 75.6 us
  waiting for transfers between devices: 46.6 us -> 0 us
  matrix products: 26.9 us -> 0 us
  between operations: 13.5 us -> 0.01 us
  other arithmetic: 7.37 us -> 0 us
    psum x1 -> x0, blocking collectives: 124 us -> none  [body(): joint_total = lax.psum(totals, 'kv')]
    pmax x1 -> x0, blocking collectives: 121 us -> none  [body(): top = lax.pmax(jnp.max(scores, axis=-1), 'kv')]
    unnamed x1 -> x0, blocking collectives: 75.6 us -> none
    pallas_call x0 -> x1, Pallas kernels: none -> 75.6 us  [body(): pl.pallas_call(kernel, out_shape=jax.ShapeDtypeStruct((ROWS, FEAT), BF),...]
    all_gather x1 -> x0, waiting for transfers between devices: 46.6 us -> none  [body(): query_group = lax.all_gather(query_mine, 'kv', axis=2, tiled=True)]
    dot_general x4 -> x0, matrix products: 26.9 us -> none  [the longest x1 14 us: body(): jnp.einsum('bsgd,bjd->bsgj', query_group, latent_cache, preferred_element...]
  transfers between devices with their start and end apart: 2 -> 0, of which waited for: 1 -> 0; matrix products, arithmetic and copies ran while one was open for 1% -> 0% of each run, Pallas kernels for 0% -> 0%
where the time goes in v2:
time: 77.3 us; the launch traced here: 76.9 us
  Pallas kernels  75.6 us (98%)
  local copies, waits for them, and re-layouts  1.31 us (2%)
    pallas_call x1, Pallas kernels, body(): pl.pallas_call(kernel, out_shape=jax.ShapeDtypeStruct((ROWS, FEAT), BF),...  75.6 us

profile of v2, /device:TPU:1, one launch (start us, length us, event | category | flops | bytes accessed | tf_op | source)
XLA Modules:
  0.0 76.9 jit_solution(5557232921912914634)
XLA Ops:
  0.0 75.6 %shard_map.73 = bf16[48,56]{1,0:T(8,128)(2,1)} custom-call(s32[16]{0:T(128)} %lengths_ref.1, s32[16]{0:T(128)} %positions_ref.1, bf16[48,192]{1,0:T(8,128)(2,1)} %bitcast.15, bf16[128,512]{1,0:T(8,128)(2,1)} %bitcast.12, bf16[512,128]{1,0:T(8,128)(2,1)} %bitcast.13, bf16[128,7168]{1,0:T(8,128)(2,1)} %weight_hbm.1, bf16[16,576,1024]{2,1,0:T(8,128)(2,1)} %bitcast.11), custom_call_target="tpu_custom_call" | custom-call | tf_op jit(solution)/shard_map/pallas_call | solution.py:447
  75.6 1.3 %copy.9 = bf16[16,3,56]{2,0,1:T(8,128)(2,1)} copy(bf16[16,3,56]{2,0,1:T(8,128)(2,1)} %bitcast.14) | data formatting | bytes 10752

commit v3 on v2

--- a/solution.py
+++ b/solution.py
@@ -49,18 +49,21 @@
     return jnp.where(lane == 0, top_high, tile)
 
 
-def spread_stats(tile):
+def spread_matrix():
     source = lax.broadcasted_iota(jnp.int32, (128, 256), 0)
     target = lax.broadcasted_iota(jnp.int32, (128, 256), 1)
     is_top = (source < 3) & (target < 128)
     is_total = (source >= 3) & (source < 5) & (target >= 128)
-    spread = jnp.where(is_top | is_total, 1.0, 0.0).astype(BF)
-    both = dot(tile.astype(BF), spread, NN)
+    return jnp.where(is_top | is_total, 1.0, 0.0).astype(BF)
+
+
+def spread_stats(tile, spread):
+    both = dot(tile.astype(BF), spread[...], NN)
     return both[:, :128], both[:, 128:]
 
 
-def join(parts):
-    stats = [spread_stats(tile) for _, tile in parts]
+def join(parts, spread):
+    stats = [spread_stats(tile, spread) for _, tile in parts]
     top = functools.reduce(jnp.maximum, [m for m, _ in stats])
     factors = [jnp.exp2((m - top) * FACTOR) for m, _ in stats]
     total = sum(f * l for f, (_, l) in zip(factors, stats))
@@ -84,7 +87,7 @@
     cache, weight, wide, wide_sib, gathered, query_f32, scores_a, scores_b, probs_a, probs_b,
     stats_a, stats_b, partial, pair_send, pair_recv, first_send, first_recv, second_send, second_recv,
     latent, values, values_sib, out_send, out_first, out_mid, out_second, out_pairs, out_third,
-    cache_sem, weight_sem, g1_send, g1_recv, g2_send, g2_recv, g3_send, g3_recv, g4_send, g4_recv,
+    spread, cache_sem, weight_sem, g1_send, g1_recv, g2_send, g2_recv, g3_send, g3_recv, g4_send, g4_recv,
     pair_ss, pair_rs, r1_send, r1_recv, r2_send, r2_recv, w_send, w_recv, v_send, v_recv,
     o1_send, o1_recv, o2_send, o2_recv, o3_send, o3_recv,
 ):
@@ -126,6 +129,8 @@
     weight_copy.start()
     for b in range(B):
         cache_copy(b).start()
+
+    spread[...] = spread_matrix()
 
     line = lax.broadcasted_iota(jnp.int32, (ROWS, ROWS), 0)
     column = lax.broadcasted_iota(jnp.int32, (ROWS, ROWS), 1)
@@ -201,20 +206,21 @@
     lax.fori_loop(0, 8, widen, 0)
     weight_send = remote(wide.at[1 - core], wide_sib, w_send.at[0], w_recv.at[0], sibling)
 
-    for k in range(CHUNKS):
+    def to_second(k):
         for step in range(1, 4):
             gather_one(k, step).wait_recv()
         for side in range(2):
             gather_two(k, side).start()
-    for k in range(CHUNKS):
+
+    def to_third(k):
         for side in range(2):
             gather_two(k, side).wait_recv()
             gather_three(k, side).start()
-    for k in range(CHUNKS):
+
+    def to_sibling(k):
         for side in range(2):
             gather_three(k, side).wait_recv()
         gather_four(k).start()
-    weight_send.start()
 
     def unpack(k):
         for parity in range(2):
@@ -223,9 +229,19 @@
                     gathered[parity, k, :, :, 128 * t : 128 * t + 128].astype(F32).reshape(256, 128)
                 )
 
-    for k in range(CHUNKS):
+    def arrive(k):
         gather_four(k).wait_recv()
         unpack(k)
+
+    to_second(0)
+    to_second(1)
+    to_third(0)
+    to_second(2)
+    to_third(1)
+    to_sibling(0)
+    to_third(2)
+    weight_send.start()
+    arrive(0)
 
     slots = lax.broadcasted_iota(jnp.int32, (1, SHARD), 1)
 
@@ -287,7 +303,7 @@
             rows = slice(64 * group, 64 * group + 64)
             own_part = (lambda t, rows=rows: partial[k, t, rows], partial[k, 4, rows])
             span = slice(4 * group, 4 * group + 4)
-            store_group(k, group, join([own_part, block_part(pair_recv, (k, span), 4)]))
+            store_group(k, group, join([own_part, block_part(pair_recv, (k, span), 4)], spread))
         for step in (2, 1, 3):
             first_copy(k, step).start()
 
@@ -304,7 +320,7 @@
             first_copy(k, step).wait_recv()
         parts = [block_part(first_send, (k, slice(0, 4)), 4)]
         parts += [block_part(first_recv, (k, step), 4) for step in range(3)]
-        tiles, top, total = join(parts)
+        tiles, top, total = join(parts, spread)
         tiles = tiles + [stat_tile(top, total)]
         for t in range(WIDE // 128):
             second_send[k, :, :, 128 * t : 128 * t + 128] = tiles[t].astype(BF).reshape(4, 16, 128)
@@ -316,7 +332,7 @@
             second_copy(k, step).wait_recv()
         parts = [block_part(second_send, (k, 0), 1)]
         parts += [block_part(second_recv, (k, step), 1) for step in range(3)]
-        tiles, _, total = join(parts)
+        tiles, _, total = join(parts, spread)
         for t in range(DC // 128):
             latent[16 * k : 16 * k + 16, 128 * t : 128 * t + 128] = (tiles[t] / total).astype(BF)
 
@@ -335,11 +351,11 @@
         score(b + 1, scores_b)
         weigh(b, probs_a, stats_a)
         soften(b + 1, scores_b, probs_b, stats_b)
-        after(b, [(10, step_pair, 1), (12, step_first, 1)])
+        after(b, [(0, to_sibling, 1), (2, to_sibling, 2), (8, arrive, 2), (8, step_first, 0), (10, step_pair, 1)])
         score(b + 2, scores_a)
         weigh(b + 1, probs_b, stats_b)
         soften(b + 2, scores_a, probs_a, stats_a)
-        after(b + 1, [(5, step_pair, 0), (7, step_first, 0), (9, step_second, 0), (13, step_last, 0)])
+        after(b + 1, [(3, arrive, 1), (5, step_pair, 0), (13, step_first, 1)])
         return carry
 
     lax.fori_loop(0, B // 2 - 1, rollout_pair, 0)
@@ -347,12 +363,14 @@
     score(B - 1, scores_b)
     weigh(B - 2, probs_a, stats_a)
     soften(B - 1, scores_b, probs_b, stats_b)
-    step_second(1)
     weigh(B - 1, probs_b, stats_b)
     step_pair(2)
+    step_second(0)
+    step_first(2)
+    step_second(1)
+    step_last(0)
+    step_second(2)
     step_last(1)
-    step_first(2)
-    step_second(2)
     step_last(2)
 
     head_values = dot(latent[...], value_ref[...], NN).astype(BF)
@@ -486,6 +504,7 @@
             vmem((3, ROWS, 256), BF),
             vmem((2, ROWS, 128), BF),
             vmem((3, ROWS, 128), BF),
+            vmem((128, 256), BF),
             dma((B,)),
             dma((1,)),
             dma((CHUNKS, 3)), dma((CHUNKS, 3)),

time: 77.3 us -> 67.2 us (0.87)
  Pallas kernels: 75.6 us -> 65.7 us
    pallas_call x1, Pallas kernels: 75.6 us -> 65.7 us  [body(): pl.pallas_call(kernel, out_shape=jax.ShapeDtypeStruct((ROWS, FEAT), BF),...]
where the time goes in v3:
time: 67.2 us; the launch traced here: 67 us
  Pallas kernels  65.7 us (98%)
  local copies, waits for them, and re-layouts  1.31 us (2%)
    pallas_call x1, Pallas kernels, body(): pl.pallas_call(kernel, out_shape=jax.ShapeDtypeStruct((ROWS, FEAT), BF),...  65.7 us

profile of v3, /device:TPU:1, one launch (start us, length us, event | category | flops | bytes accessed | tf_op | source)
XLA Modules:
  0.0 67.0 jit_solution(1296190655551613604)
XLA Ops:
  0.0 65.7 %shard_map.73 = bf16[48,56]{1,0:T(8,128)(2,1)} custom-call(s32[16]{0:T(128)} %lengths_ref.1, s32[16]{0:T(128)} %positions_ref.1, bf16[48,192]{1,0:T(8,128)(2,1)} %bitcast.15, bf16[128,512]{1,0:T(8,128)(2,1)} %bitcast.12, bf16[512,128]{1,0:T(8,128)(2,1)} %bitcast.13, bf16[128,7168]{1,0:T(8,128)(2,1)} %weight_hbm.1, bf16[16,576,1024]{2,1,0:T(8,128)(2,1)} %bitcast.11), custom_call_target="tpu_custom_call" | custom-call | tf_op jit(solution)/shard_map/pallas_call | solution.py:465
  65.7 1.3 %copy.9 = bf16[16,3,56]{2,0,1:T(8,128)(2,1)} copy(bf16[16,3,56]{2,0,1:T(8,128)(2,1)} %bitcast.14) | data formatting | bytes 10752

commit v4 on v3

--- a/solution.py
+++ b/solution.py
@@ -84,12 +84,12 @@
 
 def kernel(
     lengths_ref, positions_ref, query_ref, key_ref, value_ref, weight_hbm, cache_hbm, out_ref,
-    cache, weight, wide, wide_sib, gathered, query_f32, scores_a, scores_b, probs_a, probs_b,
+    cache, weight, wide, weights_all, gathered, query_f32, scores_a, scores_b, probs_a, probs_b,
     stats_a, stats_b, partial, pair_send, pair_recv, first_send, first_recv, second_send, second_recv,
-    latent, values, values_sib, out_send, out_first, out_mid, out_second, out_pairs, out_third,
-    spread, cache_sem, weight_sem, g1_send, g1_recv, g2_send, g2_recv, g3_send, g3_recv, g4_send, g4_recv,
+    latent, values, out_send, out_recv,
+    spread, cache_sem, weight_sem, g1_send, g1_recv, g2_send, g2_recv, g3_send, g3_recv,
     pair_ss, pair_rs, r1_send, r1_recv, r2_send, r2_recv, w_send, w_recv, v_send, v_recv,
-    o1_send, o1_recv, o2_send, o2_recv, o3_send, o3_recv,
+    o_send, o_recv,
 ):
     kv = lax.axis_index("kv")
     row_y = lax.axis_index("head")
@@ -104,8 +104,11 @@
     def along_second(step):
         return place(x + step * core, z + step * (1 - core), core, row_y)
 
-    def along_third(step):
-        return place(x, z, core, row_y + step)
+    def column_peer(peer):
+        return place(x, z, lax.rem(core + peer // 4, 2), row_y + peer % 4)
+
+    def plane_peer(peer):
+        return place(x + peer // 4, z + peer % 4, core, row_y)
 
     sibling = place(x, z, 1 - core, row_y)
 
@@ -121,9 +124,7 @@
     weight_copy = pltpu.make_async_copy(weight_hbm, weight, weight_sem.at[0])
 
     barrier = pltpu.get_barrier_semaphore()
-    partners = [sibling]
-    for step in range(1, 4):
-        partners += [along_first(step), along_second(step), along_third(step)]
+    partners = [column_peer(peer) for peer in range(1, 8)] + [plane_peer(peer) for peer in range(1, 16)]
     for partner in partners:
         pl.semaphore_signal(barrier, inc=1, device_id=partner, device_id_type=MESH)
     weight_copy.start()
@@ -166,21 +167,18 @@
             g1_send.at[k, step - 1], g1_recv.at[k, step - 1], along_first(step),
         )
 
-    def gather_two(k, side):
-        return remote(
-            gathered.at[0, k, pl.ds(0, 4)], gathered.at[0, k, pl.ds(4 if side == 0 else 12, 4)],
-            g2_send.at[k, side], g2_recv.at[k, side], along_second(1 if side == 0 else 3),
-        )
-
-    def gather_three(k, side):
-        return remote(
-            gathered.at[0, k, pl.ds(4 if side == 0 else 14, 2)],
-            gathered.at[0, k, pl.ds(8 if side == 0 else 10, 2)],
-            g3_send.at[k, side], g3_recv.at[k, side], along_second(1 if side == 0 else 3),
-        )
-
-    def gather_four(k):
-        return remote(gathered.at[0, k], gathered.at[1, k], g4_send.at[k], g4_recv.at[k], sibling)
+    def gather_two(k, step):
+        return remote(
+            gathered.at[0, k, pl.ds(0, 4)], gathered.at[0, k, pl.ds(4 * step, 4)],
+            g2_send.at[k, step - 1], g2_recv.at[k, step - 1], along_second(step),
+        )
+
+    def gather_three(k, group):
+        span = pl.ds(4 * group, 4)
+        return remote(
+            gathered.at[0, k, span], gathered.at[1, k, span],
+            g3_send.at[k, group], g3_recv.at[k, group], sibling,
+        )
 
     for k in range(CHUNKS):
         for step in range(1, 4):
@@ -192,35 +190,38 @@
         base = pl.multiple_of(g * (16 * FEAT), 128)
         strip = weight[:, pl.ds(base, 16 * FEAT)]
         gap = jnp.zeros((DN, 64 - FEAT), BF)
-        for low in range(2):
-            wx, wz = g // 2, (g % 2) * 2 + low
-            for parity in range(2):
-                slot = wz * 4 + wx if parity == 0 else wx * 4 + wz
-                for half in range(2):
-                    start = ((low * 2 + parity) * 4 + half * 2) * FEAT
-                    wide[parity, slot, :, 128 * half : 128 * half + 128] = jnp.concatenate(
-                        [strip[:, start : start + FEAT], gap,
-                         strip[:, start + FEAT : start + 2 * FEAT], gap], axis=1)
+        for parity in range(2):
+            for side in range(4):
+                start = (parity * 4 + side) * FEAT
+                wide[parity, side, :, pl.ds(pl.multiple_of(g * 128, 128), 128)] = jnp.concatenate(
+                    [strip[:, start : start + FEAT], gap,
+                     strip[:, start + 8 * FEAT : start + 9 * FEAT], gap], axis=1)
         return carry
 
     lax.fori_loop(0, 8, widen, 0)
-    weight_send = remote(wide.at[1 - core], wide_sib, w_send.at[0], w_recv.at[0], sibling)
+
+    def weight_send(peer):
+        turn, step = peer // 4, peer % 4
+        return remote(
+            wide.at[lax.rem(core + turn, 2), lax.rem(row_y + step, 4)], weights_all.at[peer],
+            w_send.at[peer - 1], w_recv.at[peer - 1], column_peer(peer),
+        )
+
+    for peer in range(1, 8):
+        weight_send(peer).start()
+    weights_all[0] = wide[core, row_y]
 
     def to_second(k):
         for step in range(1, 4):
             gather_one(k, step).wait_recv()
-        for side in range(2):
-            gather_two(k, side).start()
-
-    def to_third(k):
-        for side in range(2):
-            gather_two(k, side).wait_recv()
-            gather_three(k, side).start()
+        for step in (2, 1, 3):
+            gather_two(k, step).start()
+        gather_three(k, 0).start()
 
     def to_sibling(k):
-        for side in range(2):
-            gather_three(k, side).wait_recv()
-        gather_four(k).start()
+        for step in (1, 3, 2):
+            gather_two(k, step).wait_recv()
+            gather_three(k, step).start()
 
     def unpack(k):
         for parity in range(2):
@@ -230,17 +231,14 @@
                 )
 
     def arrive(k):
-        gather_four(k).wait_recv()
+        for group in range(4):
+            gather_three(k, group).wait_recv()
         unpack(k)
 
     to_second(0)
     to_second(1)
-    to_third(0)
+    to_sibling(0)
     to_second(2)
-    to_third(1)
-    to_sibling(0)
-    to_third(2)
-    weight_send.start()
     arrive(0)
 
     slots = lax.broadcasted_iota(jnp.int32, (1, SHARD), 1)
@@ -375,85 +373,66 @@
 
     head_values = dot(latent[...], value_ref[...], NN).astype(BF)
     back = jnp.where(line == (column % S) * B + column // S, 1.0, 0.0).astype(BF)
-    values[...] = dot(back, head_values, NN).astype(BF)
-    values_copy = remote(values, values_sib, v_send.at[0], v_recv.at[0], sibling)
-    values_copy.start()
-    weight_send.wait_recv()
-    values_copy.wait_recv()
-
-    own_second = x * core + z * (1 - core)
-    own_first = x * (1 - core) + z * core
-    both_values = jnp.concatenate([values[...], values_sib[...]], axis=1)
-
-    def project(t, carry):
-        both_weights = jnp.concatenate([wide[core, t], wide_sib[t]], axis=0)
-        out_send[t] = dot(both_values, both_weights, NN).astype(BF)
-        return carry
-
-    lax.fori_loop(0, 16, project, 0)
-
-    def out_one(step):
-        return remote(
-            out_send.at[pl.ds(4 * lax.rem(own_second + step, 4), 4)], out_first.at[step - 1],
-            o1_send.at[step - 1], o1_recv.at[step - 1], along_second(step),
-        )
-
-    def out_two(step):
-        return remote(
-            out_mid.at[lax.rem(own_first + step, 4)], out_second.at[step - 1],
-            o2_send.at[step - 1], o2_recv.at[step - 1], along_first(step),
-        )
-
-    def out_three(step):
-        return remote(
-            out_pairs.at[lax.rem(row_y + step, 4) // 2], out_third.at[step - 1],
-            o3_send.at[step - 1], o3_recv.at[step - 1], along_third(step),
-        )
-
-    for step in (2, 1, 3):
-        out_one(step).start()
-    for step in range(1, 4):
-        out_one(step).wait_recv()
-    for f in range(4):
-        total = out_send[own_second * 4 + f].astype(F32)
-        for step in range(3):
-            total = total + out_first[step, f].astype(F32)
-        out_mid[f] = total.astype(BF)
-    for step in (2, 1, 3):
-        out_two(step).start()
-    for step in range(1, 4):
-        out_two(step).wait_recv()
-    total = out_mid[own_first].astype(F32)
-    for step in range(3):
-        total = total + out_second[step].astype(F32)
-    out_pairs[0] = total[:, :128].astype(BF)
-    out_pairs[1] = total[:, 128:].astype(BF)
-    for step in (2, 1, 3):
-        out_three(step).start()
-    for step in range(1, 4):
-        out_three(step).wait_recv()
-    total = out_pairs[row_y // 2].astype(F32)
-    for step in range(3):
-        total = total + out_third[step].astype(F32)
-    mine = jnp.where(row_y % 2 == 0, total[:, :FEAT], total[:, 64 : 64 + FEAT])
-    out_ref[...] = mine.astype(BF)
+    values[0] = dot(back, head_values, NN).astype(BF)
+
+    def values_copy(peer):
+        return remote(
+            values.at[0], values.at[peer], v_send.at[peer - 1], v_recv.at[peer - 1], column_peer(peer)
+        )
+
+    for peer in range(1, 8):
+        values_copy(peer).start()
+    for peer in range(1, 8):
+        weight_send(peer).wait_recv()
+    for peer in range(1, 8):
+        values_copy(peer).wait_recv()
+
+    all_values = jnp.concatenate([values[peer] for peer in range(8)], axis=1)
+    for strip in range(4):
+        lanes = slice(256 * strip, 256 * strip + 256)
+        features = dot(all_values, weights_all[:, :, lanes].reshape(8 * DN, 256), NN)
+        for slot in range(4):
+            piece = features[:, 64 * slot : 64 * slot + 64]
+            out_send[4 * strip + slot] = jnp.concatenate(
+                [
+                    jnp.concatenate([piece[:16], piece[16:32]], axis=1),
+                    jnp.concatenate([piece[32:], jnp.zeros((16, 64), F32)], axis=1),
+                ],
+                axis=0,
+            ).astype(BF)
+
+    def out_copy(peer):
+        target = lax.rem(x + peer // 4, 4) * 4 + lax.rem(z + peer % 4, 4)
+        return remote(
+            out_send.at[target], out_recv.at[peer - 1],
+            o_send.at[peer - 1], o_recv.at[peer - 1], plane_peer(peer),
+        )
+
+    for peer in (10, 2, 8, 6, 9, 11, 14, 1, 3, 4, 5, 7, 12, 13, 15):
+        out_copy(peer).start()
+    total = out_send[x * 4 + z].astype(F32)
+    for peer in range(1, 16):
+        out_copy(peer).wait_recv()
+    for peer in range(1, 16):
+        total = total + out_recv[peer - 1].astype(F32)
+    out_ref[...] = jnp.concatenate(
+        [total[:16, :FEAT], total[:16, 64 : 64 + FEAT], total[16:, :FEAT]], axis=0
+    ).astype(BF)
 
     for k in range(CHUNKS):
         for step in range(1, 4):
             gather_one(k, step).wait_send()
             first_copy(k, step).wait_send()
             second_copy(k, step).wait_send()
-        for side in range(2):
-            gather_two(k, side).wait_send()
-            gather_three(k, side).wait_send()
-        gather_four(k).wait_send()
+            gather_two(k, step).wait_send()
+        for group in range(4):
+            gather_three(k, group).wait_send()
         pair_copy(k).wait_send()
-    weight_send.wait_send()
-    values_copy.wait_send()
-    for step in range(1, 4):
-        out_one(step).wait_send()
-        out_two(step).wait_send()
-        out_three(step).wait_send()
+    for peer in range(1, 8):
+        weight_send(peer).wait_send()
+        values_copy(peer).wait_send()
+    for peer in range(1, 16):
+        out_copy(peer).wait_send()
 
 
 def body(query_heads, key_up, value_up, output_weight, latent_cache, lengths, positions):
@@ -478,8 +457,8 @@
         scratch_shapes=[
             vmem((B, RANK, SHARD), BF),
             vmem((DN, width), BF),
-            vmem((2, 16, DN, 256), BF),
-            vmem((16, DN, 256), BF),
+            vmem((2, 4, DN, 1024), BF),
+            vmem((8, DN, 1024), BF),
             vmem((2, CHUNKS, 16, 16, WIDE), BF),
             vmem((CHUNKS, WIDE // 128, 512, 128), F32),
             vmem((96, SHARD), F32),
@@ -496,29 +475,21 @@
             vmem((CHUNKS, 4, 16, WIDE), BF),
             vmem((CHUNKS, 3, 16, WIDE), BF),
             vmem((ROWS, DC), BF),
-            vmem((ROWS, 128), BF),
-            vmem((ROWS, 128), BF),
-            vmem((16, ROWS, 256), BF),
-            vmem((3, 4, ROWS, 256), BF),
-            vmem((4, ROWS, 256), BF),
-            vmem((3, ROWS, 256), BF),
-            vmem((2, ROWS, 128), BF),
-            vmem((3, ROWS, 128), BF),
+            vmem((8, ROWS, 128), BF),
+            vmem((16, 32, 128), BF),
+            vmem((15, 32, 128), BF),
             vmem((128, 256), BF),
             dma((B,)),
             dma((1,)),
             dma((CHUNKS, 3)), dma((CHUNKS, 3)),
-            dma((CHUNKS, 2)), dma((CHUNKS, 2)),
-            dma((CHUNKS, 2)), dma((CHUNKS, 2)),
-            dma((CHUNKS,)), dma((CHUNKS,)),
+            dma((CHUNKS, 3)), dma((CHUNKS, 3)),
+            dma((CHUNKS, 4)), dma((CHUNKS, 4)),
             dma((CHUNKS,)), dma((CHUNKS,)),
             dma((CHUNKS, 3)), dma((CHUNKS, 3)),
             dma((CHUNKS, 3)), dma((CHUNKS, 3)),
-            dma((1,)), dma((1,)),
-            dma((1,)), dma((1,)),
-            dma((3,)), dma((3,)),
-            dma((3,)), dma((3,)),
-            dma((3,)), dma((3,)),
+            dma((7,)), dma((7,)),
+            dma((7,)), dma((7,)),
+            dma((15,)), dma((15,)),
         ],
         compiler_params=pltpu.CompilerParams(
             collective_id=0, has_side_effects=True, vmem_limit_bytes=56 * 2**20

time: 67.2 us -> 60 us (0.89)
  Pallas kernels: 65.7 us -> 58.5 us
    pallas_call x1, Pallas kernels: 65.7 us -> 58.5 us  [body(): pl.pallas_call(kernel, out_shape=jax.ShapeDtypeStruct((ROWS, FEAT), BF),...]
where the time goes in v4:
time: 60 us; the launch traced here: 59.8 us
  Pallas kernels  58.5 us (98%)
  local copies, waits for them, and re-layouts  1.31 us (2%)
    pallas_call x1, Pallas kernels, body(): pl.pallas_call(kernel, out_shape=jax.ShapeDtypeStruct((ROWS, FEAT), BF),...  58.5 us
    unnamed x1, local copies, waits for them, and re-layouts  1.31 us

profile of v4, /device:TPU:1, one launch (start us, length us, event | category | flops | bytes accessed | tf_op | source)
XLA Modules:
  0.0 59.8 jit_solution(14464109677143429099)
XLA Ops:
  0.0 58.5 %shard_map.73 = bf16[48,56]{1,0:T(8,128)(2,1)} custom-call(s32[16]{0:T(128)} %lengths_ref.1, s32[16]{0:T(128)} %positions_ref.1, bf16[48,192]{1,0:T(8,128)(2,1)} %bitcast.15, bf16[128,512]{1,0:T(8,128)(2,1)} %bitcast.12, bf16[512,128]{1,0:T(8,128)(2,1)} %bitcast.13, bf16[128,7168]{1,0:T(8,128)(2,1)} %weight_hbm.1, bf16[16,576,1024]{2,1,0:T(8,128)(2,1)} %bitcast.11), custom_call_target="tpu_custom_call" | custom-call | tf_op jit(solution)/shard_map/pallas_call | solution.py:444
  58.5 1.3 %copy.9 = bf16[16,3,56]{2,0,1:T(8,128)(2,1)} copy(bf16[16,3,56]{2,0,1:T(8,128)(2,1)} %bitcast.14) | data formatting | bytes 10752

commit v5 on v4

--- a/solution.py
+++ b/solution.py
@@ -24,6 +24,7 @@
 SHARD = 1024
 FEAT = 56
 MASKED = -(2.0**100)
+PLANE_ORDER = (10, 6, 9, 11, 14, 2, 8, 5, 7, 13, 15, 1, 3, 4, 12)
 FACTOR = float(np.log2(np.e) / np.sqrt(DN + DR))
 
 dot = functools.partial(lax.dot_general, preferred_element_type=F32)
@@ -73,6 +74,20 @@
     return tiles, top, total
 
 
+def join_stack(ref, spread):
+    count = ref.shape[0]
+    tops, totals = spread_stats(ref[:, :, DC:].reshape(count * 16, 128), spread)
+    tops = tops.reshape(count, 16, 128)
+    top = jnp.max(tops, axis=0)
+    factors = jnp.exp2((tops - top[None]) * FACTOR)
+    total = jnp.sum(factors * totals.reshape(count, 16, 128), axis=0)
+    tiles = [
+        jnp.sum(factors * ref[:, :, 128 * t : 128 * t + 128].astype(F32), axis=0)
+        for t in range(DC // 128)
+    ]
+    return tiles, top, total
+
+
 def block_part(ref, index, count):
     rows = count * 16
 
@@ -83,13 +98,13 @@
 
 
 def kernel(
-    lengths_ref, positions_ref, query_ref, key_ref, value_ref, weight_hbm, cache_hbm, out_ref,
+    lengths_hbm, positions_hbm, query_hbm, key_hbm, value_hbm, weight_hbm, cache_hbm, out_ref,
+    lengths_ref, positions_ref, query_ref, key_ref, value_ref,
     cache, weight, wide, weights_all, gathered, query_f32, scores_a, scores_b, probs_a, probs_b,
     stats_a, stats_b, partial, pair_send, pair_recv, first_send, first_recv, second_send, second_recv,
     latent, values, out_send, out_recv,
-    spread, cache_sem, weight_sem, g1_send, g1_recv, g2_send, g2_recv, g3_send, g3_recv,
-    pair_ss, pair_rs, r1_send, r1_recv, r2_send, r2_recv, w_send, w_recv, v_send, v_recv,
-    o_send, o_recv,
+    last_recv, spread, cache_sem, small_sem, g1_send, g1_recv, g2_send, g2_recv, g3_send, g3_recv,
+    pair_ss, pair_rs, r1_send, r1_recv, r2_send, r2_recv, w_send, w_recv, v_send, v_recv, o_send, o_recv,
 ):
     kv = lax.axis_index("kv")
     row_y = lax.axis_index("head")
@@ -99,16 +114,19 @@
         return (lax.rem(px, 4) * 8 + lax.rem(pz, 4) * 2 + pc, lax.rem(py, 4))
 
     def along_first(step):
-        return place(x + step * (1 - core), z + step * core, core, row_y)
+        return plane_peer(step)
 
     def along_second(step):
-        return place(x + step * core, z + step * (1 - core), core, row_y)
+        return plane_peer(4 * step)
 
     def column_peer(peer):
         return place(x, z, lax.rem(core + peer // 4, 2), row_y + peer % 4)
 
     def plane_peer(peer):
-        return place(x + peer // 4, z + peer % 4, core, row_y)
+        first, second = peer % 4, peer // 4
+        return place(
+            x + first * (1 - core) + second * core, z + second * (1 - core) + first * core, core, row_y
+        )
 
     sibling = place(x, z, 1 - core, row_y)
 
@@ -118,21 +136,37 @@
             device_id=device, device_id_type=MESH,
         )
 
-    def cache_copy(b):
-        return pltpu.make_async_copy(cache_hbm.at[b], cache.at[b], cache_sem.at[b])
-
-    weight_copy = pltpu.make_async_copy(weight_hbm, weight, weight_sem.at[0])
+    def arrived(ref, semaphore):
+        remote(ref, ref, semaphore, semaphore, sibling).wait_recv()
+
+    def departed(ref, semaphore):
+        remote(ref, ref, semaphore, semaphore, sibling).wait_send()
+
+    def cache_copy(pair):
+        span = pl.ds(2 * pair, 2)
+        return pltpu.make_async_copy(cache_hbm.at[span], cache.at[span], cache_sem.at[pair])
+
+    small_copies = [
+        pltpu.make_async_copy(source, target, small_sem.at[i])
+        for i, (source, target) in enumerate([
+            (positions_hbm, positions_ref), (query_hbm, query_ref), (key_hbm, key_ref),
+            (lengths_hbm, lengths_ref), (weight_hbm, weight), (value_hbm, value_ref),
+        ])
+    ]
 
     barrier = pltpu.get_barrier_semaphore()
-    partners = [column_peer(peer) for peer in range(1, 8)] + [plane_peer(peer) for peer in range(1, 16)]
+    partners = [plane_peer(peer) for peer in PLANE_ORDER] + [column_peer(peer) for peer in range(1, 8)]
     for partner in partners:
         pl.semaphore_signal(barrier, inc=1, device_id=partner, device_id_type=MESH)
-    weight_copy.start()
-    for b in range(B):
-        cache_copy(b).start()
+    for copy in small_copies:
+        copy.start()
+    for pair in range(B // 2):
+        cache_copy(pair).start()
 
     spread[...] = spread_matrix()
 
+    for copy in small_copies[:4]:
+        copy.wait()
     line = lax.broadcasted_iota(jnp.int32, (ROWS, ROWS), 0)
     column = lax.broadcasted_iota(jnp.int32, (ROWS, ROWS), 1)
     reorder = jnp.where(column == (line % S) * B + line // S, 1.0, 0.0).astype(BF)
@@ -161,30 +195,31 @@
 
     pl.semaphore_wait(barrier, len(partners))
 
-    def gather_one(k, step):
-        return remote(
-            gathered.at[0, k, 0], gathered.at[0, k, step],
-            g1_send.at[k, step - 1], g1_recv.at[k, step - 1], along_first(step),
+    def gather_one(k, peer):
+        return remote(
+            gathered.at[0, k, 0], gathered.at[0, k, peer], g1_send.at[k],
+            g1_recv.at[CHUNKS if k == 0 and peer >= 8 else k], plane_peer(peer),
         )
 
     def gather_two(k, step):
         return remote(
             gathered.at[0, k, pl.ds(0, 4)], gathered.at[0, k, pl.ds(4 * step, 4)],
-            g2_send.at[k, step - 1], g2_recv.at[k, step - 1], along_second(step),
-        )
-
-    def gather_three(k, group):
-        span = pl.ds(4 * group, 4)
-        return remote(
-            gathered.at[0, k, span], gathered.at[1, k, span],
-            g3_send.at[k, group], g3_recv.at[k, group], sibling,
-        )
-
-    for k in range(CHUNKS):
-        for step in range(1, 4):
+            g2_send.at[k], g2_recv.at[k], along_second(step),
+        )
+
+    def gather_three(k, start, count):
+        span = pl.ds(start, count)
+        return remote(
+            gathered.at[0, k, span], gathered.at[1, k, span], g3_send.at[k], g3_recv.at[k], sibling
+        )
+
+    for peer in (2, 5, 6, 7, 1, 3, 4, 10, 8, 9, 11, 14, 13, 15, 12):
+        gather_one(0, peer).start()
+    for k in range(1, CHUNKS):
+        for step in (2, 1, 3):
             gather_one(k, step).start()
 
-    weight_copy.wait()
+    small_copies[4].wait()
 
     def widen(g, carry):
         base = pl.multiple_of(g * (16 * FEAT), 128)
@@ -204,7 +239,7 @@
         turn, step = peer // 4, peer % 4
         return remote(
             wide.at[lax.rem(core + turn, 2), lax.rem(row_y + step, 4)], weights_all.at[peer],
-            w_send.at[peer - 1], w_recv.at[peer - 1], column_peer(peer),
+            w_send.at[0], w_recv.at[0], column_peer(peer),
         )
 
     for peer in range(1, 8):
@@ -212,16 +247,14 @@
     weights_all[0] = wide[core, row_y]
 
     def to_second(k):
-        for step in range(1, 4):
-            gather_one(k, step).wait_recv()
+        arrived(gathered.at[0, k, pl.ds(1, 3)], g1_recv.at[k])
         for step in (2, 1, 3):
             gather_two(k, step).start()
-        gather_three(k, 0).start()
+        gather_three(k, 0, 4).start()
 
     def to_sibling(k):
-        for step in (1, 3, 2):
-            gather_two(k, step).wait_recv()
-            gather_three(k, step).start()
+        arrived(gathered.at[0, k, pl.ds(4, 12)], g2_recv.at[k])
+        gather_three(k, 4, 12).start()
 
     def unpack(k):
         for parity in range(2):
@@ -231,13 +264,14 @@
                 )
 
     def arrive(k):
-        for group in range(4):
-            gather_three(k, group).wait_recv()
+        arrived(gathered.at[1, k], g3_recv.at[k])
         unpack(k)
 
-    to_second(0)
+    arrived(gathered.at[0, 0, pl.ds(1, 7)], g1_recv.at[0])
+    gather_three(0, 0, 8).start()
+    arrived(gathered.at[0, 0, pl.ds(8, 8)], g1_recv.at[CHUNKS])
+    gather_three(0, 8, 8).start()
     to_second(1)
-    to_sibling(0)
     to_second(2)
     arrive(0)
 
@@ -279,13 +313,13 @@
     def first_copy(k, step):
         return remote(
             first_send.at[k, pl.ds(4 * step, 4)], first_recv.at[k, step - 1],
-            r1_send.at[k, step - 1], r1_recv.at[k, step - 1], along_second(4 - step),
+            r1_send.at[k], r1_recv.at[k], along_second(4 - step),
         )
 
     def second_copy(k, step):
         return remote(
             second_send.at[k, step], second_recv.at[k, step - 1],
-            r2_send.at[k, step - 1], r2_recv.at[k, step - 1], along_first(4 - step),
+            r2_send.at[k], r2_recv.at[k], along_first(4 - step),
         )
 
     def step_pair(k):
@@ -302,8 +336,20 @@
             own_part = (lambda t, rows=rows: partial[k, t, rows], partial[k, 4, rows])
             span = slice(4 * group, 4 * group + 4)
             store_group(k, group, join([own_part, block_part(pair_recv, (k, span), 4)], spread))
-        for step in (2, 1, 3):
-            first_copy(k, step).start()
+        if k < CHUNKS - 1:
+            for step in (2, 1, 3):
+                first_copy(k, step).start()
+        else:
+            for peer in PLANE_ORDER:
+                last_copy(peer).start()
+            last_recv[0] = first_send[k, 0]
+
+    def last_copy(peer):
+        back = (4 - peer // 4) % 4 * 4 + (4 - peer % 4) % 4
+        return remote(
+            first_send.at[CHUNKS - 1, peer], last_recv.at[peer],
+            r1_send.at[CHUNKS - 1], r1_recv.at[CHUNKS - 1], plane_peer(back),
+        )
 
     def store_group(k, group, joined):
         tiles, top, total = joined
@@ -314,8 +360,7 @@
             )
 
     def step_second(k):
-        for step in range(1, 4):
-            first_copy(k, step).wait_recv()
+        arrived(first_recv.at[k], r1_recv.at[k])
         parts = [block_part(first_send, (k, slice(0, 4)), 4)]
         parts += [block_part(first_recv, (k, step), 4) for step in range(3)]
         tiles, top, total = join(parts, spread)
@@ -326,11 +371,14 @@
             second_copy(k, step).start()
 
     def step_last(k):
-        for step in range(1, 4):
-            second_copy(k, step).wait_recv()
-        parts = [block_part(second_send, (k, 0), 1)]
-        parts += [block_part(second_recv, (k, step), 1) for step in range(3)]
-        tiles, _, total = join(parts, spread)
+        if k < CHUNKS - 1:
+            arrived(second_recv.at[k], r2_recv.at[k])
+            parts = [block_part(second_send, (k, 0), 1)]
+            parts += [block_part(second_recv, (k, step), 1) for step in range(3)]
+            tiles, _, total = join(parts, spread)
+        else:
+            arrived(last_recv.at[pl.ds(1, 15)], r1_recv.at[k])
+            tiles, _, total = join_stack(last_recv, spread)
         for t in range(DC // 128):
             latent[16 * k : 16 * k + 16, 128 * t : 128 * t + 128] = (tiles[t] / total).astype(BF)
 
@@ -344,8 +392,7 @@
 
     def rollout_pair(i, carry):
         b = 2 * i
-        cache_copy(b + 1).wait()
-        cache_copy(b + 2).wait()
+        cache_copy(i + 1).wait()
         score(b + 1, scores_b)
         weigh(b, probs_a, stats_a)
         soften(b + 1, scores_b, probs_b, stats_b)
@@ -357,7 +404,6 @@
         return carry
 
     lax.fori_loop(0, B // 2 - 1, rollout_pair, 0)
-    cache_copy(B - 1).wait()
     score(B - 1, scores_b)
     weigh(B - 2, probs_a, stats_a)
     soften(B - 1, scores_b, probs_b, stats_b)
@@ -367,9 +413,10 @@
     step_first(2)
     step_second(1)
     step_last(0)
-    step_second(2)
     step_last(1)
     step_last(2)
+
+    small_copies[5].wait()
 
     head_values = dot(latent[...], value_ref[...], NN).astype(BF)
     back = jnp.where(line == (column % S) * B + column // S, 1.0, 0.0).astype(BF)
@@ -377,15 +424,13 @@
 
     def values_copy(peer):
         return remote(
-            values.at[0], values.at[peer], v_send.at[peer - 1], v_recv.at[peer - 1], column_peer(peer)
+            values.at[0], values.at[peer], v_send.at[0], v_recv.at[0], column_peer(peer)
         )
 
     for peer in range(1, 8):
         values_copy(peer).start()
-    for peer in range(1, 8):
-        weight_send(peer).wait_recv()
-    for peer in range(1, 8):
-        values_copy(peer).wait_recv()
+    arrived(weights_all.at[pl.ds(1, 7)], w_recv.at[0])
+    arrived(values.at[pl.ds(1, 7)], v_recv.at[0])
 
     all_values = jnp.concatenate([values[peer] for peer in range(8)], axis=1)
     for strip in range(4):
@@ -402,17 +447,19 @@
             ).astype(BF)
 
     def out_copy(peer):
-        target = lax.rem(x + peer // 4, 4) * 4 + lax.rem(z + peer % 4, 4)
+        first, second = peer % 4, peer // 4
+        target = lax.rem(x + first * (1 - core) + second * core, 4) * 4 + lax.rem(
+            z + second * (1 - core) + first * core, 4
+        )
         return remote(
             out_send.at[target], out_recv.at[peer - 1],
-            o_send.at[peer - 1], o_recv.at[peer - 1], plane_peer(peer),
-        )
-
-    for peer in (10, 2, 8, 6, 9, 11, 14, 1, 3, 4, 5, 7, 12, 13, 15):
+            o_send.at[0], o_recv.at[0], plane_peer(peer),
+        )
+
+    for peer in PLANE_ORDER:
         out_copy(peer).start()
     total = out_send[x * 4 + z].astype(F32)
-    for peer in range(1, 16):
-        out_copy(peer).wait_recv()
+    arrived(out_recv, o_recv.at[0])
     for peer in range(1, 16):
         total = total + out_recv[peer - 1].astype(F32)
     out_ref[...] = jnp.concatenate(
@@ -420,19 +467,19 @@
     ).astype(BF)
 
     for k in range(CHUNKS):
-        for step in range(1, 4):
-            gather_one(k, step).wait_send()
-            first_copy(k, step).wait_send()
-            second_copy(k, step).wait_send()
-            gather_two(k, step).wait_send()
-        for group in range(4):
-            gather_three(k, group).wait_send()
-        pair_copy(k).wait_send()
-    for peer in range(1, 8):
-        weight_send(peer).wait_send()
-        values_copy(peer).wait_send()
-    for peer in range(1, 16):
-        out_copy(peer).wait_send()
+        departed(gathered.at[0, k, pl.ds(1, 15 if k == 0 else 3)], g1_send.at[k])
+        departed(gathered.at[0, k], g3_send.at[k])
+        departed(pair_recv.at[k], pair_ss.at[k])
+        if k > 0:
+            departed(gathered.at[0, k, pl.ds(4, 12)], g2_send.at[k])
+        if k < CHUNKS - 1:
+            departed(first_recv.at[k], r1_send.at[k])
+            departed(second_recv.at[k], r2_send.at[k])
+        else:
+            departed(last_recv.at[pl.ds(1, 15)], r1_send.at[k])
+    departed(weights_all.at[pl.ds(1, 7)], w_send.at[0])
+    departed(values.at[pl.ds(1, 7)], v_send.at[0])
+    departed(out_recv, o_send.at[0])
 
 
 def body(query_heads, key_up, value_up, output_weight, latent_cache, lengths, positions):
@@ -445,16 +492,15 @@
         kernel,
         out_shape=jax.ShapeDtypeStruct((ROWS, FEAT), BF),
         in_specs=[
-            pl.BlockSpec(memory_space=smem),
-            pl.BlockSpec(memory_space=smem),
-            pl.BlockSpec(memory_space=vmem),
-            pl.BlockSpec(memory_space=vmem),
-            pl.BlockSpec(memory_space=vmem),
-            pl.BlockSpec(memory_space=pl.ANY),
-            pl.BlockSpec(memory_space=pl.ANY),
+            pl.BlockSpec(memory_space=pl.ANY) for _ in range(7)
         ],
         out_specs=pl.BlockSpec(memory_space=vmem),
         scratch_shapes=[
+            smem((B,), jnp.int32),
+            smem((B,), jnp.int32),
+            vmem((ROWS, DN + DR), BF),
+            vmem((DN, DC), BF),
+            vmem((DC, 128), BF),
             vmem((B, RANK, SHARD), BF),
             vmem((DN, width), BF),
             vmem((2, 4, DN, 1024), BF),
@@ -478,18 +524,19 @@
             vmem((8, ROWS, 128), BF),
             vmem((16, 32, 128), BF),
             vmem((15, 32, 128), BF),
+            vmem((16, 16, WIDE), BF),
             vmem((128, 256), BF),
-            dma((B,)),
-            dma((1,)),
-            dma((CHUNKS, 3)), dma((CHUNKS, 3)),
-            dma((CHUNKS, 3)), dma((CHUNKS, 3)),
-            dma((CHUNKS, 4)), dma((CHUNKS, 4)),
+            dma((B // 2,)),
+            dma((6,)),
+            dma((CHUNKS,)), dma((CHUNKS + 1,)),
             dma((CHUNKS,)), dma((CHUNKS,)),
-            dma((CHUNKS, 3)), dma((CHUNKS, 3)),
-            dma((CHUNKS, 3)), dma((CHUNKS, 3)),
-            dma((7,)), dma((7,)),
-            dma((7,)), dma((7,)),
-            dma((15,)), dma((15,)),
+            dma((CHUNKS,)), dma((CHUNKS,)),
+            dma((CHUNKS,)), dma((CHUNKS,)),
+            dma((CHUNKS,)), dma((CHUNKS,)),
+            dma((CHUNKS,)), dma((CHUNKS,)),
+            dma((1,)), dma((1,)),
+            dma((1,)), dma((1,)),
+            dma((1,)), dma((1,)),
         ],
         compiler_params=pltpu.CompilerParams(
             collective_id=0, has_side_effects=True, vmem_limit_bytes=56 * 2**20

time: 60 us -> 54.9 us (0.915)
  Pallas kernels: 58.5 us -> 53.4 us
    pallas_call x1, Pallas kernels: 58.5 us -> 53.4 us  [body(): pl.pallas_call(kernel, out_shape=jax.ShapeDtypeStruct((ROWS, FEAT), BF),...]
where the time goes in v5:
time: 54.9 us; the launch traced here: 54.7 us
  Pallas kernels  53.4 us (97%)
  local copies, waits for them, and re-layouts  1.31 us (2%)
    pallas_call x1, Pallas kernels, body(): pl.pallas_call(kernel, out_shape=jax.ShapeDtypeStruct((ROWS, FEAT), BF),...  53.4 us
    unnamed x1, local copies, waits for them, and re-layouts  1.31 us

profile of v5, /device:TPU:1, one launch (start us, length us, event | category | flops | bytes accessed | tf_op | source)
XLA Modules:
  0.0 54.7 jit_solution(13909558024388023364)
XLA Ops:
  0.0 53.4 %shard_map.73 = bf16[48,56]{1,0:T(8,128)(2,1)} custom-call(s32[16]{0:T(128)} %lengths_hbm.1, s32[16]{0:T(128)} %positions_hbm.1, bf16[48,192]{1,0:T(8,128)(2,1)} %bitcast.15, bf16[128,512]{1,0:T(8,128)(2,1)} %bitcast.12, bf16[512,128]{1,0:T(8,128)(2,1)} %bitcast.13, bf16[128,7168]{1,0:T(8,128)(2,1)} %weight_hbm.1, bf16[16,576,1024]{2,1,0:T(8,128)(2,1)} %bitcast.11), custom_call_target="tpu_custom_call" | custom-call | tf_op jit(solution)/shard_map/pallas_call | solution.py:491
  53.4 1.3 %copy.9 = bf16[16,3,56]{2,0,1:T(8,128)(2,1)} copy(bf16[16,3,56]{2,0,1:T(8,128)(2,1)} %bitcast.14) | data formatting | bytes 10752

commit v6 on v5

--- a/solution.py
+++ b/solution.py
@@ -213,11 +213,12 @@
             gathered.at[0, k, span], gathered.at[1, k, span], g3_send.at[k], g3_recv.at[k], sibling
         )
 
+    for step in (2, 1, 3):
+        gather_one(1, step).start()
     for peer in (2, 5, 6, 7, 1, 3, 4, 10, 8, 9, 11, 14, 13, 15, 12):
         gather_one(0, peer).start()
-    for k in range(1, CHUNKS):
-        for step in (2, 1, 3):
-            gather_one(k, step).start()
+    for step in (2, 1, 3):
+        gather_one(2, step).start()
 
     small_copies[4].wait()
 
@@ -267,11 +268,11 @@
         arrived(gathered.at[1, k], g3_recv.at[k])
         unpack(k)
 
+    to_second(1)
     arrived(gathered.at[0, 0, pl.ds(1, 7)], g1_recv.at[0])
     gather_three(0, 0, 8).start()
     arrived(gathered.at[0, 0, pl.ds(8, 8)], g1_recv.at[CHUNKS])
     gather_three(0, 8, 8).start()
-    to_second(1)
     to_second(2)
     arrive(0)
 
@@ -307,8 +308,11 @@
                 ]
             partial[r // 16, 4, pl.ds(r % 16, 32, stride=16), :] = stats[32 * s : 32 * s + 32, :]
 
-    def pair_copy(k):
-        return remote(pair_send.at[k], pair_recv.at[k], pair_ss.at[k], pair_rs.at[k], sibling)
+    def pair_copy(k, start, count, channel):
+        span = pl.ds(start, count)
+        return remote(
+            pair_send.at[k, span], pair_recv.at[k, span], pair_ss.at[k], pair_rs.at[channel], sibling
+        )
 
     def first_copy(k, step):
         return remote(
@@ -321,28 +325,6 @@
             second_send.at[k, step], second_recv.at[k, step - 1],
             r2_send.at[k], r2_recv.at[k], along_first(4 - step),
         )
-
-    def step_pair(k):
-        for t in range(WIDE // 128):
-            pair_send[k, :, :, 128 * t : 128 * t + 128] = (
-                partial[k, t, 256:512].astype(BF).reshape(16, 16, 128)
-            )
-        pair_copy(k).start()
-
-    def step_first(k):
-        pair_copy(k).wait_recv()
-        for group in range(4):
-            rows = slice(64 * group, 64 * group + 64)
-            own_part = (lambda t, rows=rows: partial[k, t, rows], partial[k, 4, rows])
-            span = slice(4 * group, 4 * group + 4)
-            store_group(k, group, join([own_part, block_part(pair_recv, (k, span), 4)], spread))
-        if k < CHUNKS - 1:
-            for step in (2, 1, 3):
-                first_copy(k, step).start()
-        else:
-            for peer in PLANE_ORDER:
-                last_copy(peer).start()
-            last_recv[0] = first_send[k, 0]
 
     def last_copy(peer):
         back = (4 - peer // 4) % 4 * 4 + (4 - peer % 4) % 4
@@ -358,6 +340,44 @@
             first_send[k, 4 * group : 4 * group + 4, :, 128 * t : 128 * t + 128] = (
                 tiles[t].astype(BF).reshape(4, 16, 128)
             )
+
+    def pack_pair(k, start, count):
+        for t in range(WIDE // 128):
+            pair_send[k, start : start + count, :, 128 * t : 128 * t + 128] = (
+                partial[k, t, 256 + 16 * start : 256 + 16 * (start + count)]
+                .astype(BF)
+                .reshape(count, 16, 128)
+            )
+
+    def step_pair(k):
+        pack_pair(k, 0, 16)
+        pair_copy(k, 0, 16, k).start()
+
+    def join_group(k, group):
+        rows = slice(64 * group, 64 * group + 64)
+        span = slice(4 * group, 4 * group + 4)
+        own_part = (lambda t: partial[k, t, rows], partial[k, 4, rows])
+        store_group(k, group, join([own_part, block_part(pair_recv, (k, span), 4)], spread))
+
+    def step_first(k):
+        arrived(pair_recv.at[k], pair_rs.at[k])
+        for group in range(4):
+            join_group(k, group)
+        for step in (2, 1, 3):
+            first_copy(k, step).start()
+
+    def last_pair():
+        for group in (2, 1, 3, 0):
+            pack_pair(CHUNKS - 1, 4 * group, 4)
+            pair_copy(CHUNKS - 1, 4 * group, 4, CHUNKS - 1 + group).start()
+
+    def last_first():
+        for group in (2, 1, 3, 0):
+            arrived(pair_recv.at[CHUNKS - 1, pl.ds(4 * group, 4)], pair_rs.at[CHUNKS - 1 + group])
+            join_group(CHUNKS - 1, group)
+            for peer in range(max(1, 4 * group), 4 * group + 4):
+                last_copy(peer).start()
+        last_recv[0] = first_send[CHUNKS - 1, 0]
 
     def step_second(k):
         arrived(first_recv.at[k], r1_recv.at[k])
@@ -396,11 +416,11 @@
         score(b + 1, scores_b)
         weigh(b, probs_a, stats_a)
         soften(b + 1, scores_b, probs_b, stats_b)
-        after(b, [(0, to_sibling, 1), (2, to_sibling, 2), (8, arrive, 2), (8, step_first, 0), (10, step_pair, 1)])
+        after(b, [(6, to_sibling, 2), (8, arrive, 2), (8, step_first, 0), (10, step_pair, 1)])
         score(b + 2, scores_a)
         weigh(b + 1, probs_b, stats_b)
         soften(b + 2, scores_a, probs_a, stats_a)
-        after(b + 1, [(3, arrive, 1), (5, step_pair, 0), (13, step_first, 1)])
+        after(b + 1, [(1, to_sibling, 1), (3, arrive, 1), (5, step_pair, 0), (13, step_first, 1)])
         return carry
 
     lax.fori_loop(0, B // 2 - 1, rollout_pair, 0)
@@ -408,9 +428,9 @@
     weigh(B - 2, probs_a, stats_a)
     soften(B - 1, scores_b, probs_b, stats_b)
     weigh(B - 1, probs_b, stats_b)
-    step_pair(2)
+    last_pair()
     step_second(0)
-    step_first(2)
+    last_first()
     step_second(1)
     step_last(0)
     step_last(1)
@@ -433,32 +453,28 @@
     arrived(values.at[pl.ds(1, 7)], v_recv.at[0])
 
     all_values = jnp.concatenate([values[peer] for peer in range(8)], axis=1)
-    for strip in range(4):
-        lanes = slice(256 * strip, 256 * strip + 256)
+    def out_copy(over, beside):
+        return remote(
+            out_send.at[over, lax.rem(z + beside, 4)], out_recv.at[4 * over + beside - 1],
+            o_send.at[0], o_recv.at[0], place(x + over, z + beside, core, row_y),
+        )
+
+    for over in (2, 1, 3, 0):
+        lanes = pl.ds(pl.multiple_of(256 * lax.rem(x + over, 4), 256), 256)
         features = dot(all_values, weights_all[:, :, lanes].reshape(8 * DN, 256), NN)
         for slot in range(4):
             piece = features[:, 64 * slot : 64 * slot + 64]
-            out_send[4 * strip + slot] = jnp.concatenate(
+            out_send[over, slot] = jnp.concatenate(
                 [
                     jnp.concatenate([piece[:16], piece[16:32]], axis=1),
                     jnp.concatenate([piece[32:], jnp.zeros((16, 64), F32)], axis=1),
                 ],
                 axis=0,
             ).astype(BF)
-
-    def out_copy(peer):
-        first, second = peer % 4, peer // 4
-        target = lax.rem(x + first * (1 - core) + second * core, 4) * 4 + lax.rem(
-            z + second * (1 - core) + first * core, 4
-        )
-        return remote(
-            out_send.at[target], out_recv.at[peer - 1],
-            o_send.at[0], o_recv.at[0], plane_peer(peer),
-        )
-
-    for peer in PLANE_ORDER:
-        out_copy(peer).start()
-    total = out_send[x * 4 + z].astype(F32)
+        for beside in (2, 1, 3, 0):
+            if over or beside:
+                out_copy(over, beside).start()
+    total = out_send[0, z].astype(F32)
     arrived(out_recv, o_recv.at[0])
     for peer in range(1, 16):
         total = total + out_recv[peer - 1].astype(F32)
@@ -522,7 +538,7 @@
             vmem((CHUNKS, 3, 16, WIDE), BF),
             vmem((ROWS, DC), BF),
             vmem((8, ROWS, 128), BF),
-            vmem((16, 32, 128), BF),
+            vmem((4, 4, 32, 128), BF),
             vmem((15, 32, 128), BF),
             vmem((16, 16, WIDE), BF),
             vmem((128, 256), BF),
@@ -531,7 +547,7 @@
             dma((CHUNKS,)), dma((CHUNKS + 1,)),
             dma((CHUNKS,)), dma((CHUNKS,)),
             dma((CHUNKS,)), dma((CHUNKS,)),
-            dma((CHUNKS,)), dma((CHUNKS,)),
+            dma((CHUNKS,)), dma((CHUNKS + 3,)),
             dma((CHUNKS,)), dma((CHUNKS,)),
             dma((CHUNKS,)), dma((CHUNKS,)),
             dma((1,)), dma((1,)),

time: 54.9 us -> 53.6 us (0.976)
  Pallas kernels: 53.4 us -> 52.1 us
    pallas_call x1, Pallas kernels: 53.4 us -> 52.1 us  [body(): pl.pallas_call(kernel, out_shape=jax.ShapeDtypeStruct((ROWS, FEAT), BF),...]
where the time goes in v6:
time: 53.6 us; the launch traced here: 53.5 us
  Pallas kernels  52.1 us (97%)
  local copies, waits for them, and re-layouts  1.31 us (2%)
    pallas_call x1, Pallas kernels, body(): pl.pallas_call(kernel, out_shape=jax.ShapeDtypeStruct((ROWS, FEAT), BF),...  52.1 us
    unnamed x1, local copies, waits for them, and re-layouts  1.31 us

profile of v6, /device:TPU:1, one launch (start us, length us, event | category | flops | bytes accessed | tf_op | source)
XLA Modules:
  0.0 53.5 jit_solution(9599506713020574767)
XLA Ops:
  0.0 52.1 %shard_map.73 = bf16[48,56]{1,0:T(8,128)(2,1)} custom-call(s32[16]{0:T(128)} %lengths_hbm.1, s32[16]{0:T(128)} %positions_hbm.1, bf16[48,192]{1,0:T(8,128)(2,1)} %bitcast.15, bf16[128,512]{1,0:T(8,128)(2,1)} %bitcast.12, bf16[512,128]{1,0:T(8,128)(2,1)} %bitcast.13, bf16[128,7168]{1,0:T(8,128)(2,1)} %weight_hbm.1, bf16[16,576,1024]{2,1,0:T(8,128)(2,1)} %bitcast.11), custom_call_target="tpu_custom_call" | custom-call | tf_op jit(solution)/shard_map/pallas_call | solution.py:507
  52.2 1.3 %copy.9 = bf16[16,3,56]{2,0,1:T(8,128)(2,1)} copy(bf16[16,3,56]{2,0,1:T(8,128)(2,1)} %bitcast.14) | data formatting | bytes 10752

commit v7 on v6

--- a/solution.py
+++ b/solution.py
@@ -257,16 +257,16 @@
         arrived(gathered.at[0, k, pl.ds(4, 12)], g2_recv.at[k])
         gather_three(k, 4, 12).start()
 
-    def unpack(k):
-        for parity in range(2):
-            for t in range(WIDE // 128):
-                query_f32[k, t, parity * 256 : parity * 256 + 256] = (
-                    gathered[parity, k, :, :, 128 * t : 128 * t + 128].astype(F32).reshape(256, 128)
-                )
+    def unpack(k, parity):
+        for t in range(WIDE // 128):
+            query_f32[k, t, parity * 256 : parity * 256 + 256] = (
+                gathered[parity, k, :, :, 128 * t : 128 * t + 128].astype(F32).reshape(256, 128)
+            )
 
     def arrive(k):
+        unpack(k, 0)
         arrived(gathered.at[1, k], g3_recv.at[k])
-        unpack(k)
+        unpack(k, 1)
 
     to_second(1)
     arrived(gathered.at[0, 0, pl.ds(1, 7)], g1_recv.at[0])
@@ -408,7 +408,8 @@
 
     def after(b, schedule):
         for when, step, k in schedule:
-            pl.when(b == when)(functools.partial(step, k))
+            if b == when:
+                step(k)
 
     def rollout_pair(i, carry):
         b = 2 * i
@@ -423,7 +424,8 @@
         after(b + 1, [(1, to_sibling, 1), (3, arrive, 1), (5, step_pair, 0), (13, step_first, 1)])
         return carry
 
-    lax.fori_loop(0, B // 2 - 1, rollout_pair, 0)
+    for i in range(B // 2 - 1):
+        rollout_pair(i, 0)
     score(B - 1, scores_b)
     weigh(B - 2, probs_a, stats_a)
     soften(B - 1, scores_b, probs_b, stats_b)

time: 53.6 us -> 52.4 us (0.978)
  Pallas kernels: 52.1 us -> 51 us
    pallas_call x1, Pallas kernels: 52.1 us -> 51 us  [body(): pl.pallas_call(kernel, out_shape=jax.ShapeDtypeStruct((ROWS, FEAT), BF),...]
where the time goes in v7:
time: 52.4 us; the launch traced here: 52.3 us
  Pallas kernels  51 us (97%)
  local copies, waits for them, and re-layouts  1.31 us (2%)
    pallas_call x1, Pallas kernels, body(): pl.pallas_call(kernel, out_shape=jax.ShapeDtypeStruct((ROWS, FEAT), BF),...  51 us
    unnamed x1, local copies, waits for them, and re-layouts  1.31 us

profile of v7, /device:TPU:1, one launch (start us, length us, event | category | flops | bytes accessed | tf_op | source)
XLA Modules:
  0.0 52.3 jit_solution(13278973246438164121)
XLA Ops:
  0.0 51.0 %shard_map.73 = bf16[48,56]{1,0:T(8,128)(2,1)} custom-call(s32[16]{0:T(128)} %lengths_hbm.1, s32[16]{0:T(128)} %positions_hbm.1, bf16[48,192]{1,0:T(8,128)(2,1)} %bitcast.15, bf16[128,512]{1,0:T(8,128)(2,1)} %bitcast.12, bf16[512,128]{1,0:T(8,128)(2,1)} %bitcast.13, bf16[128,7168]{1,0:T(8,128)(2,1)} %weight_hbm.1, bf16[16,576,1024]{2,1,0:T(8,128)(2,1)} %bitcast.11), custom_call_target="tpu_custom_call" | custom-call | tf_op jit(solution)/shard_map/pallas_call | solution.py:509
  51.0 1.3 %copy.9 = bf16[16,3,56]{2,0,1:T(8,128)(2,1)} copy(bf16[16,3,56]{2,0,1:T(8,128)(2,1)} %bitcast.14) | data formatting | bytes 10752

commit v8 on v7

--- a/solution.py
+++ b/solution.py
@@ -417,11 +417,11 @@
         score(b + 1, scores_b)
         weigh(b, probs_a, stats_a)
         soften(b + 1, scores_b, probs_b, stats_b)
-        after(b, [(6, to_sibling, 2), (8, arrive, 2), (8, step_first, 0), (10, step_pair, 1)])
+        after(b, [(6, to_sibling, 2), (8, arrive, 2), (8, step_first, 0), (10, step_pair, 1), (12, step_first, 1)])
         score(b + 2, scores_a)
         weigh(b + 1, probs_b, stats_b)
         soften(b + 2, scores_a, probs_a, stats_a)
-        after(b + 1, [(1, to_sibling, 1), (3, arrive, 1), (5, step_pair, 0), (13, step_first, 1)])
+        after(b + 1, [(1, to_sibling, 1), (3, arrive, 1), (5, step_pair, 0)])
         return carry
 
     for i in range(B // 2 - 1):

time: 52.4 us -> 51.9 us (level)
  no operation moved by 1% of the time
where the time goes in v8:
time: 51.9 us; the launch traced here: 51.8 us
  Pallas kernels  50.5 us (97%)
  local copies, waits for them, and re-layouts  1.31 us (3%)
    pallas_call x1, Pallas kernels, body(): pl.pallas_call(kernel, out_shape=jax.ShapeDtypeStruct((ROWS, FEAT), BF),...  50.5 us
    unnamed x1, local copies, waits for them, and re-layouts  1.31 us

profile of v8, /device:TPU:1, one launch (start us, length us, event | category | flops | bytes accessed | tf_op | source)
XLA Modules:
  0.0 51.8 jit_solution(712786487524789248)
XLA Ops:
  0.0 50.5 %shard_map.73 = bf16[48,56]{1,0:T(8,128)(2,1)} custom-call(s32[16]{0:T(128)} %lengths_hbm.1, s32[16]{0:T(128)} %positions_hbm.1, bf16[48,192]{1,0:T(8,128)(2,1)} %bitcast.15, bf16[128,512]{1,0:T(8,128)(2,1)} %bitcast.12, bf16[512,128]{1,0:T(8,128)(2,1)} %bitcast.13, bf16[128,7168]{1,0:T(8,128)(2,1)} %weight_hbm.1, bf16[16,576,1024]{2,1,0:T(8,128)(2,1)} %bitcast.11), custom_call_target="tpu_custom_call" | custom-call | tf_op jit(solution)/shard_map/pallas_call | solution.py:509
  50.5 1.3 %copy.9 = bf16[16,3,56]{2,0,1:T(8,128)(2,1)} copy(bf16[16,3,56]{2,0,1:T(8,128)(2,1)} %bitcast.14) | data formatting | bytes 10752
